TPU v7x, 32 devices: a whole 2x2x4 slice. The times are simulated.
32 devices in a mesh: section: 2 (over x), dp: 4 (over z), tensor: 4 (over y, core).
Axes of the slice: x: 2, y: 2, z: 4, core: 2. Of those that a mesh axis runs over, the one named last changes fastest.
Arguments:
- tokens: bfloat16 [8, 2048, 768], P('dp', 'tensor'), may hold values from -6 to 6
- qkv_weight: bfloat16 [2, 3, 768, 768], P('section', None, None, 'tensor'), may hold values from -0.21875 to 0.21875
- out_weight: bfloat16 [2, 768, 768], P('section', 'tensor'), may hold values from -2.5 to 2.5
- up_weight: bfloat16 [2, 768, 3072], P('section', None, 'tensor'), may hold values from -0.21875 to 0.21875
- down_weight: bfloat16 [2, 3072, 768], P('section', 'tensor'), may hold values from -0.109375 to 0.109375
- vectors: float32 [2, 3, 768], P('section'), may hold values from -4 to 4
- lengths: int32 [8], P('dp'), may hold values from 1024 to 2048, as said below
- selected: int32 [8, 256], P('dp'), may hold values from 0 to 2047, as said below
- cotangent: bfloat16 [8, 2048, 768], P('dp', 'tensor'), may hold values from -6 to 6
Outputs:
- section_results: float32 [2, 8, 2048, 768], P('section', 'dp', 'tensor')
- qkv_grad: float32 [2, 3, 768, 768], P('section', None, 'dp', 'tensor')
- out_proj_grad: float32 [2, 768, 768], P('section', 'tensor', 'dp')
- up_grad: float32 [2, 768, 3072], P('section', 'dp', 'tensor')
- down_grad: float32 [2, 3072, 768], P('section', 'tensor', 'dp')
- vector_grad: float32 [2, 3, 768], P('section', None, 'dp')
Inputs may be any that keep to these rules, and one draw needn't show every extreme that they name: `lengths`: in each group of 2 consecutive sequences one has length 2048; every length is at least half of 2048. `selected`: each row holds 256 distinct positions in increasing order, all below that sequence's length.
All inputs are finite; a program needn't handle non-finite values.
Results may differ from a plain program's by a relative error of at most 0.02.
Values may be sent and summed in bfloat16 or wider, within the bound.
No kernel may reach another device: no remote copies, remote signals or barrier semaphores. Data moves between devices by JAX's collectives and lax.ppermute only.
A program may use at most 256 MiB of HBM per device.

v0:
```python
import jax
import jax.numpy as jnp
from jax import lax
from jax.sharding import PartitionSpec as P

HEADS = 12


EPSILON = 1e-06
PRECISE = lax.Precision.HIGHEST
NEGATIVE = -1e30


def as_sent(shard):
    return jax.tree.map(lambda a: a.astype(jnp.bfloat16) if a.dtype == jnp.float32 else a, shard)


def passed_along(block, axis, distance):
    devices = range(lax.axis_size(axis))
    route = [(i - distance, i) for i in devices if i - distance in devices]
    return lax.ppermute(block, axis, route)


def norm_rows(values, gain):
    return values * lax.rsqrt(jnp.mean(values * values, axis=-1, keepdims=True) + EPSILON) * gain


def spread_rows(values):
    return lax.all_gather(values, "tensor", axis=0, tiled=True)


def spread_grads(values):
    return jax.tree.map(
        lambda part, own: part.astype(own.dtype),
        lax.all_gather(as_sent(values), "tensor", axis=0, tiled=True),
        values,
    )


def gather_sums(term, row_count):
    return lax.psum_scatter(
        term(jnp.int32(0), row_count * lax.axis_size("tensor")).astype(jnp.bfloat16),
        "tensor",
        scatter_dimension=0,
        tiled=True,
    ).astype(jnp.float32)


def gather_grad_sums(term, row_count):
    return lax.psum_scatter(
        term(jnp.int32(0), row_count * lax.axis_size("tensor")).astype(jnp.bfloat16),
        "tensor",
        scatter_dimension=0,
        tiled=True,
    ).astype(jnp.float32)


def reduce_grads(grads):
    return (
        lax.psum_scatter(
            grads[0].astype(jnp.bfloat16), "dp", scatter_dimension=1, tiled=True
        ).astype(jnp.float32),
        lax.psum_scatter(
            grads[1].astype(jnp.bfloat16), "dp", scatter_dimension=1, tiled=True
        ).astype(jnp.float32),
        lax.psum_scatter(
            grads[2].astype(jnp.bfloat16), "dp", scatter_dimension=0, tiled=True
        ).astype(jnp.float32),
        lax.psum_scatter(
            grads[3].astype(jnp.bfloat16), "dp", scatter_dimension=1, tiled=True
        ).astype(jnp.float32),
        lax.psum_scatter(
            grads[4].astype(jnp.bfloat16), "dp", scatter_dimension=1, tiled=True
        ).astype(jnp.float32),
    )


def split_heads(packed, head_count):
    row_count = packed.shape[1]
    width = packed.shape[2] // head_count
    return (
        packed[0].reshape(row_count, head_count, width),
        packed[1].reshape(row_count, head_count, width),
        packed[2].reshape(row_count, head_count, width),
    )


def masked_scores(query_block, keys_all, places, opening, span_rows, length):
    score_scale = keys_all.shape[2] ** (-0.5)
    allowed = (places[None, :] <= places[opening : opening + span_rows, None]) & (places < length)[
        None, :
    ]
    scores = (
        jnp.einsum("qhd,khd->hqk", query_block, keys_all, preferred_element_type=jnp.float32)
        * score_scale
    )
    return jnp.where(allowed[None], scores, NEGATIVE)


def attention_forward(packed, places, length, head_count):
    row_count = packed.shape[1]
    queries, keys_all, values_all = split_heads(packed, head_count)
    span_rows = min(512, row_count)
    mixed_parts = []
    total_parts = []
    for opening in range(0, row_count, span_rows):
        scores = masked_scores(
            queries[opening : opening + span_rows], keys_all, places, opening, span_rows, length
        )
        highest = jnp.max(scores, axis=-1, keepdims=True)
        expos = jnp.exp(scores - highest)
        totals = jnp.sum(expos, axis=-1, keepdims=True)
        probs = (expos / totals).astype(jnp.bfloat16)
        mixed = jnp.einsum("hqk,khd->qhd", probs, values_all, preferred_element_type=jnp.float32)
        mixed_parts.append(mixed.reshape(span_rows, packed.shape[2]))
        total_parts.append((highest + jnp.log(totals))[..., 0])
    return (jnp.concatenate(mixed_parts, 0).astype(jnp.bfloat16), jnp.concatenate(total_parts, 1))


def attention_backward(packed, log_totals, grad_mixed, places, length, head_count):
    row_count = packed.shape[1]
    queries, keys_all, values_all = split_heads(packed, head_count)
    width = keys_all.shape[2]
    score_scale = width ** (-0.5)
    grad_heads = grad_mixed.reshape(row_count, head_count, width)
    span_rows = min(512, row_count)
    key_grad = jnp.zeros((row_count, head_count, width), jnp.float32)
    value_grad = jnp.zeros((row_count, head_count, width), jnp.float32)
    query_parts = []
    for opening in range(0, row_count, span_rows):
        query_block = queries[opening : opening + span_rows]
        grad_block = grad_heads[opening : opening + span_rows]
        scores = masked_scores(query_block, keys_all, places, opening, span_rows, length)
        probs = jnp.exp(scores - log_totals[:, opening : opening + span_rows, None])
        prob_grad = jnp.einsum(
            "qhd,khd->hqk", grad_block, values_all, preferred_element_type=jnp.float32
        )
        inner = jnp.sum(probs * prob_grad, axis=-1, keepdims=True)
        score_grad = (probs * (prob_grad - inner) * score_scale).astype(jnp.bfloat16)
        query_parts.append(
            jnp.einsum("hqk,khd->qhd", score_grad, keys_all, preferred_element_type=jnp.float32)
        )
        key_grad = key_grad + jnp.einsum(
            "hqk,qhd->khd", score_grad, query_block, preferred_element_type=jnp.float32
        )
        value_grad = value_grad + jnp.einsum(
            "hqk,qhd->khd",
            probs.astype(jnp.bfloat16),
            grad_block,
            preferred_element_type=jnp.float32,
        )
    query_grad = jnp.concatenate(query_parts, 0)
    flat_width = head_count * width
    return jnp.stack(
        [
            query_grad.reshape(row_count, flat_width),
            key_grad.reshape(row_count, flat_width),
            value_grad.reshape(row_count, flat_width),
        ]
    ).astype(jnp.bfloat16)


def layer_forward(own_rows, gains, weights, places, length, head_count):
    packed_weight, mix_weight, widen_weight, narrow_weight = weights
    own_count = own_rows.shape[0]
    normed = spread_rows(norm_rows(own_rows, gains[0]).astype(jnp.bfloat16))
    packed = jnp.einsum(
        "rd,kdc->krc", normed, packed_weight, preferred_element_type=jnp.float32
    ).astype(jnp.bfloat16)
    mixed, log_totals = attention_forward(packed, places, length, head_count)

    def attn_term(offset, row_span):
        return jnp.dot(
            lax.dynamic_slice_in_dim(mixed, offset, row_span, 0),
            mix_weight,
            preferred_element_type=jnp.float32,
        )

    attn = gather_sums(attn_term, own_count)
    middle = own_rows + attn
    normed_two = spread_rows(norm_rows(middle, gains[1]).astype(jnp.bfloat16))
    pre = jnp.dot(normed_two, widen_weight, preferred_element_type=jnp.float32)
    act = jax.nn.gelu(pre).astype(jnp.bfloat16)

    def mlp_term(offset, row_span):
        return jnp.dot(
            lax.dynamic_slice_in_dim(act, offset, row_span, 0),
            narrow_weight,
            preferred_element_type=jnp.float32,
        )

    mlp = gather_sums(mlp_term, own_count)
    kept = (normed, packed, mixed, log_totals, middle, normed_two, pre, act)
    return (attn, mlp, middle, kept)


def layer_backward(
    own_rows, gains, weights, places, length, head_count, kept, d_attn, d_mlp, d_middle
):
    packed_weight, mix_weight, widen_weight, narrow_weight = weights
    normed, packed, mixed, log_totals, middle, normed_two, pre, act = kept
    own_count = own_rows.shape[0]
    mlp_rows = spread_grads(d_mlp.astype(jnp.bfloat16))
    d_act = jnp.einsum("rd,fd->rf", mlp_rows, narrow_weight, preferred_element_type=jnp.float32)
    grad_narrow = jnp.einsum("rf,rd->fd", act, mlp_rows, preferred_element_type=jnp.float32)
    unused, gelu_back = jax.vjp(jax.nn.gelu, pre)
    d_pre = gelu_back(d_act)[0].astype(jnp.bfloat16)
    grad_widen = jnp.einsum("rd,rf->df", normed_two, d_pre, preferred_element_type=jnp.float32)

    def widen_term(offset, row_span):
        return jnp.einsum(
            "rf,df->rd",
            lax.dynamic_slice_in_dim(d_pre, offset, row_span, 0),
            widen_weight,
            preferred_element_type=jnp.float32,
        )

    d_second = gather_grad_sums(widen_term, own_count)
    unused_two, second_back = jax.vjp(norm_rows, middle, gains[1])
    d_mid_norm, grad_gain_two = second_back(d_second)
    d_middle = d_middle + d_mid_norm
    attn_rows = spread_grads((d_attn + d_middle).astype(jnp.bfloat16))
    d_mixed = jnp.einsum(
        "rd,cd->rc", attn_rows, mix_weight, preferred_element_type=jnp.float32
    ).astype(jnp.bfloat16)
    grad_mix = jnp.einsum("rc,rd->cd", mixed, attn_rows, preferred_element_type=jnp.float32)
    d_packed = attention_backward(packed, log_totals, d_mixed, places, length, head_count)
    grad_packed = jnp.einsum("rd,krc->kdc", normed, d_packed, preferred_element_type=jnp.float32)

    def packed_term(offset, row_span):
        return jnp.einsum(
            "krc,kdc->rd",
            lax.dynamic_slice_in_dim(d_packed, offset, row_span, 1),
            packed_weight,
            preferred_element_type=jnp.float32,
        )

    d_first = gather_grad_sums(packed_term, own_count)
    unused_three, first_back = jax.vjp(norm_rows, own_rows, gains[0])
    d_own_norm, grad_gain_one = first_back(d_first)
    return (
        d_middle + d_own_norm,
        (grad_packed, grad_mix, grad_widen, grad_narrow),
        grad_gain_one,
        grad_gain_two,
    )


def local_positions(own_count):
    return jnp.arange(own_count, dtype=jnp.int32) + lax.axis_index("tensor") * own_count


def routed_forward(own_rows, places, length, gains, weights, head_count):
    own_count = own_rows.shape[0]
    local = local_positions(own_count)
    pick_count = places.shape[0] // lax.axis_size("tensor")

    def pick_term(offset, row_span):
        chosen = lax.dynamic_slice_in_dim(places, offset, row_span, 0)
        table = (chosen[:, None] == local[None, :]).astype(jnp.bfloat16)
        return jnp.dot(table, own_rows, preferred_element_type=jnp.float32)

    picked = lax.psum_scatter(
        pick_term(jnp.int32(0), pick_count * lax.axis_size("tensor")).astype(jnp.bfloat16),
        "tensor",
        scatter_dimension=0,
        tiled=True,
    ).astype(jnp.float32)
    router_scale = picked.shape[1] ** (-0.5)
    router = jnp.dot(picked, gains[2], precision=PRECISE) * router_scale
    attn, mlp, middle, kept = layer_forward(picked, gains, weights, places, length, head_count)
    update = router[:, None] * (attn + mlp)
    return (picked, router, attn, mlp, kept, update)


def place_updates(own_rows, update, places):
    local = local_positions(own_rows.shape[0])
    incoming = lax.all_gather(as_sent(update), "tensor", axis=0, tiled=True)
    chosen = lax.dynamic_slice_in_dim(places, jnp.int32(0), incoming.shape[0], 0)
    table = (chosen[:, None] == local[None, :]).astype(jnp.float32)
    return own_rows.astype(jnp.float32) + jnp.einsum(
        "cs,cd->sd", table, incoming, precision=PRECISE
    )


def routed_backward(own_rows, layer_grad, places, length, gains, weights, head_count):
    picked, router, attn, mlp, kept, unused = routed_forward(
        own_rows, places, length, gains, weights, head_count
    )
    router_scale = picked.shape[1] ** (-0.5)
    local = local_positions(own_rows.shape[0])
    pick_count = places.shape[0] // lax.axis_size("tensor")

    def pick_term(offset, row_span):
        chosen = lax.dynamic_slice_in_dim(places, offset, row_span, 0)
        table = (chosen[:, None] == local[None, :]).astype(jnp.bfloat16)
        return jnp.dot(table, layer_grad, preferred_element_type=jnp.float32)

    d_sel = lax.psum_scatter(
        pick_term(jnp.int32(0), pick_count * lax.axis_size("tensor")).astype(jnp.bfloat16),
        "tensor",
        scatter_dimension=0,
        tiled=True,
    ).astype(jnp.float32)
    scaled = router[:, None] * d_sel
    d_router = jnp.sum(d_sel * (attn + mlp), axis=1)
    d_own, weight_grads, grad_gain_one, grad_gain_two = layer_backward(
        picked,
        gains,
        weights,
        places,
        length,
        head_count,
        kept,
        scaled,
        scaled,
        jnp.zeros_like(scaled),
    )
    d_picked = (d_own + d_router[:, None] * (gains[2] * router_scale)[None, :]).astype(jnp.bfloat16)
    grad_router = jnp.dot(d_router, picked, precision=PRECISE) * router_scale
    incoming = lax.all_gather(d_picked, "tensor", axis=0, tiled=True)
    chosen = lax.dynamic_slice_in_dim(places, jnp.int32(0), incoming.shape[0], 0)
    table = (chosen[:, None] == local[None, :]).astype(jnp.bfloat16)
    input_grad = layer_grad.astype(jnp.float32) + jnp.einsum(
        "cs,cd->sd", table, incoming, preferred_element_type=jnp.float32
    )
    return (input_grad, weight_grads, jnp.stack([grad_gain_one, grad_gain_two, grad_router]))


def dense_pass(layer_input, outer_grad, length, gains, weights, head_count):
    row_count = layer_input.shape[0] * lax.axis_size("tensor")
    places = jnp.arange(row_count, dtype=jnp.int32)
    attn, mlp, middle, kept = layer_forward(layer_input, gains, weights, places, length, head_count)
    result, final_back = jax.vjp(norm_rows, middle + mlp, gains[2])
    d_final, grad_final = final_back(outer_grad.astype(jnp.float32))
    d_input, weight_grads, grad_gain_one, grad_gain_two = layer_backward(
        layer_input,
        gains,
        weights,
        places,
        length,
        head_count,
        kept,
        jnp.zeros_like(d_final),
        d_final,
        d_final,
    )
    return (
        result,
        d_input.astype(jnp.bfloat16),
        weight_grads,
        jnp.stack([grad_gain_one, grad_gain_two, grad_final]),
    )


def add_tuples(earlier, later):
    return tuple((left_part + right_part for left_part, right_part in zip(earlier, later)))


def pick_tuples(flag, first, second):
    return tuple(
        (jnp.where(flag, left_part, right_part) for left_part, right_part in zip(first, second))
    )


def body(
    tokens, qkv_weight, out_weight, up_weight, down_weight, vectors, lengths, selected, cotangent
):
    section_index = lax.axis_index("section")
    head_count = HEADS // lax.axis_size("tensor")
    weights = (qkv_weight[0], out_weight[0], up_weight[0], down_weight[0])
    gains = vectors[0]
    grad_layouts = tuple((weight.shape for weight in weights)) + (gains.shape,)

    def blank_grads():
        return tuple((jnp.zeros(layout, jnp.float32) for layout in grad_layouts))

    def step_send(running, element):
        own_rows, places, length = element
        update = routed_forward(own_rows, places, length, gains, weights, head_count)[5]
        return (running, place_updates(own_rows, update, places).astype(jnp.bfloat16))

    payload = lax.scan(step_send, jnp.float32(0), (tokens, selected, lengths))[1]
    arrived = passed_along(payload, "section", 1)

    def step_dense(running, element):
        own_rows, places, length, incoming, outer_grad = element
        layer_input = incoming.astype(jnp.float32)
        result, input_grad, weight_grads, vector_grads = dense_pass(
            layer_input, outer_grad, length, gains, weights, head_count
        )
        grads = weight_grads + (vector_grads,)
        return (add_tuples(running, grads), (result, input_grad))

    dense_grads, outcome = lax.scan(
        step_dense, blank_grads(), (tokens, selected, lengths, arrived, cotangent)
    )
    results, layer_grads = outcome
    returned = passed_along(layer_grads, "section", -1)

    def step_routed(running, element):
        own_rows, places, length, layer_grad = element
        input_grad, weight_grads, vector_grads = routed_backward(
            own_rows, layer_grad, places, length, gains, weights, head_count
        )
        grads = weight_grads + (vector_grads,)
        return (add_tuples(running, grads), input_grad)

    routed_grads, input_grads = lax.scan(
        step_routed, blank_grads(), (tokens, selected, lengths, returned)
    )
    is_routed = section_index == 0
    combined = jnp.where(is_routed, input_grads, results)
    totals = pick_tuples(is_routed, routed_grads, dense_grads)
    reduced = reduce_grads(totals)
    vector_total = lax.psum(reduced[4], "tensor")
    return (
        combined[None],
        reduced[0][None],
        reduced[1][None],
        reduced[2][None],
        reduced[3][None],
        vector_total[None],
    )


def solution(mesh):
    placed = (
        P("dp", "tensor", None),
        P("section", None, None, "tensor"),
        P("section", "tensor", None),
        P("section", None, "tensor"),
        P("section", "tensor", None),
        P("section", None, None),
        P("dp"),
        P("dp", None),
        P("dp", "tensor", None),
    )
    return jax.shard_map(
        body,
        mesh=mesh,
        in_specs=placed,
        out_specs=(
            P("section", "dp", "tensor", None),
            P("section", None, "dp", "tensor"),
            P("section", "tensor", "dp"),
            P("section", "dp", "tensor"),
            P("section", "tensor", "dp"),
            P("section", None, "dp"),
        ),
        check_vma=False,
    )
```

profile of v0, /device:TPU:0, one launch (start us, length us, event | category | flops | bytes accessed | tf_op | source)
XLA Modules:
  0.0 2078.2 jit_solution(7736268350424501944)
XLA Ops:
  9.9 209.8 %while.58 = (s32[]{:T(128)}, bf16[2,512,768]{2,1,0:T(8,128)(2,1)}, bf16[2,512,768]{2,1,0:T(8,128)(2,1)}, s32[2,256]{1,0:T(2,128)}, f32[3,768]{1,0:T(4,128)S(1)},...) while((s32[]{:T(128)}, bf16[2,512,768]{2,1,0:T(8,128)(2,1)}, ...), condition=%wide.region_8.9_spmd, body=%wide.region_0.8_spmd.sunk | while | flops 1391741184 | bytes 32884196 | solution.py:383
  15.2 23.4 %reduce-scatter.35.cloned.1.call-done = bf16[64,768]{1,0:T(8,128)(2,1)} async-done(((bf16[256,768]{1,0:T(8,128)(2,1)}), bf16[64,768]{1,0:T(8,128)(2,1)}) %reduce-scatter.35.cloned.1.call-update) | async-done | bytes 98320 | tf_op jit(solution)/shard_map/while/body/eval_jaxpr/reduce_scatter | solution.py:263
  53.0 21.2 %reduce-scatter.37.cloned.1.call-done = bf16[64,768]{1,0:T(8,128)(2,1)} async-done(((bf16[256,768]{1,0:T(8,128)(2,1)}), bf16[64,768]{1,0:T(8,128)(2,1)}) %reduce-scatter.37.cloned.1.call-update) | async-done | bytes 98320 | tf_op jit(solution)/shard_map/while/body/eval_jaxpr/reduce_scatter | solution.py:41
  85.6 21.2 %reduce-scatter.39.cloned.1.call-done = bf16[64,768]{1,0:T(8,128)(2,1)} async-done(((bf16[256,768]{1,0:T(8,128)(2,1)}), bf16[64,768]{1,0:T(8,128)(2,1)}) %reduce-scatter.39.cloned.1.call-update) | async-done | bytes 98320 | tf_op jit(solution)/shard_map/while/body/eval_jaxpr/reduce_scatter | solution.py:41
  121.2 21.1 %reduce-scatter.35.cloned.1.call-done = bf16[64,768]{1,0:T(8,128)(2,1)} async-done(((bf16[256,768]{1,0:T(8,128)(2,1)}), bf16[64,768]{1,0:T(8,128)(2,1)}) %reduce-scatter.35.cloned.1.call-update) | async-done | bytes 98320 | tf_op jit(solution)/shard_map/while/body/eval_jaxpr/reduce_scatter | solution.py:263
  156.7 21.2 %reduce-scatter.37.cloned.1.call-done = bf16[64,768]{1,0:T(8,128)(2,1)} async-done(((bf16[256,768]{1,0:T(8,128)(2,1)}), bf16[64,768]{1,0:T(8,128)(2,1)}) %reduce-scatter.37.cloned.1.call-update) | async-done | bytes 98320 | tf_op jit(solution)/shard_map/while/body/eval_jaxpr/reduce_scatter | solution.py:41
  189.3 21.2 %reduce-scatter.39.cloned.1.call-done = bf16[64,768]{1,0:T(8,128)(2,1)} async-done(((bf16[256,768]{1,0:T(8,128)(2,1)}), bf16[64,768]{1,0:T(8,128)(2,1)}) %reduce-scatter.39.cloned.1.call-update) | async-done | bytes 98320 | tf_op jit(solution)/shard_map/while/body/eval_jaxpr/reduce_scatter | solution.py:41
  223.3 34.3 %collective-permute-done = bf16[2,512,768]{2,1,0:T(8,128)(2,1)S(1)} collective-permute-done((bf16[2,512,768]{2,1,0:T(8,128)(2,1)}, bf16[2,512,768]{2,1,0:T(8,128)(2,1)S(1)}, u32[]{:S(2)}, u32[]{:S(2)}) %collective-permute-start) | collective-permute-done | bytes 1572896 | tf_op jit(solution)/shard_map/ppermute | solution.py:21
  260.7 1274.6 %while.59 = (s32[]{:T(128)}, f32[3,768,192]{1,2,0:T(8,128)}, f32[192,768]{1,0:T(8,128)}, f32[768,768]{1,0:T(8,128)}, f32[768,768]{1,0:T(8,128)}, /*index=5*/f32[...) while((s32[]{:T(128)}, f32[3,768,192]{1,2,0:T(8,128)}, ...), condition=%wide.region_35.36_spmd.clone, body=%wide.region_9.35_spmd.clone.sunk | while | flops 32022904832 | bytes 1236649088 | solution.py:395
  268.5 25.1 %all-gather.5.cloned.1.call-done = bf16[2048,768]{1,0:T(8,128)(2,1)} async-done(((bf16[512,768]{1,0:T(8,128)(2,1)}), bf16[2048,768]{1,0:T(8,128)(2,1)}) %all-gather.5.cloned.1.call-update) | async-done | bytes 3145744 | tf_op jit(solution)/shard_map/while/body/eval_jaxpr/all_gather | solution.py:29
  345.7 37.9 %reduce-scatter.41.cloned.1.call-done = bf16[512,768]{1,0:T(8,128)(2,1)} async-done(((bf16[2048,768]{1,0:T(8,128)(2,1)}), bf16[512,768]{1,0:T(8,128)(2,1)}) %reduce-scatter.41.cloned.1.call-update) | async-done | bytes 786448 | tf_op jit(solution)/shard_map/while/body/eval_jaxpr/reduce_scatter | solution.py:41
  387.4 28.6 %all-gather.7.cloned.1.call-done = bf16[2048,768]{1,0:T(8,128)(2,1)} async-done(((bf16[512,768]{1,0:T(8,128)(2,1)}), bf16[2048,768]{1,0:T(8,128)(2,1)}) %all-gather.7.cloned.1.call-update) | async-done | bytes 3145744 | tf_op jit(solution)/shard_map/while/body/eval_jaxpr/all_gather | solution.py:29
  428.9 38.1 %reduce-scatter.43.cloned.1.call-done = bf16[512,768]{1,0:T(8,128)(2,1)} async-done(((bf16[2048,768]{1,0:T(8,128)(2,1)}), bf16[512,768]{1,0:T(8,128)(2,1)}) %reduce-scatter.43.cloned.1.call-update) | async-done | bytes 786448 | tf_op jit(solution)/shard_map/while/body/eval_jaxpr/reduce_scatter | solution.py:41
  474.3 28.6 %all-gather.9.cloned.1.call-done = bf16[2048,768]{1,0:T(8,128)(2,1)} async-done(((bf16[512,768]{1,0:T(8,128)(2,1)}), bf16[2048,768]{1,0:T(8,128)(2,1)}) %all-gather.9.cloned.1.call-update) | async-done | bytes 3145744 | tf_op jit(solution)/shard_map/while/body/eval_jaxpr/all_gather | solution.py:35
  517.6 37.7 %reduce-scatter.45.cloned.1.call-done = bf16[512,768]{1,0:T(8,128)(2,1)} async-done(((bf16[2048,768]{1,0:T(8,128)(2,1)}), bf16[512,768]{1,0:T(8,128)(2,1)}) %reduce-scatter.45.cloned.1.call-update) | async-done | bytes 786448 | tf_op jit(solution)/shard_map/while/body/eval_jaxpr/reduce_scatter | solution.py:50
  563.6 26.8 %all-gather.11.cloned.1.call-done = bf16[2048,768]{1,0:T(8,128)(2,1)} async-done(((bf16[512,768]{1,0:T(8,128)(2,1)}), bf16[2048,768]{1,0:T(8,128)(2,1)}) %all-gather.11.cloned.1.call-update) | async-done | bytes 3145744 | tf_op jit(solution)/shard_map/while/body/eval_jaxpr/all_gather | solution.py:35
  600.6 24.2 %fusion.839 = bf16[512,3,64]{0,2,1:T(8,128)(2,1)} fusion(bf16[2048,3,64]{0,2,1:T(8,128)(2,1)} %bitcast.686, f32[3,512,2048]{2,1,0:T(8,128)} %fusion.828, f32[3,512,2048]{2,1,0:T(8,128)} %copy-done.5, f32[3,512]{1,0:T(4,128)} %log_add_fusion.12, pred[512,2048]{1,0:T(8,128)(4,1)} %get-tuple-element.1059), kind=kOutput, calls=%fused_computation.245.clone.1 | convolution fusion | flops 437358080 | bytes 27203584 | tf_op jit(solution)/shard_map/while/body/eval_jaxpr/hqk,khd->qhd/dot_general | solution.py:141
  624.8 27.7 %fusion.829 = f32[3,64,2048]{2,1,0:T(8,128)} fusion(bf16[512,3,64]{0,2,1:T(8,128)(2,1)} %bitcast.711, f32[3,512,2048]{2,1,0:T(8,128)} %fusion.828, f32[3,512,2048]{2,1,0:T(8,128)} %copy-done.5, f32[3,512]{1,0:T(4,128)} %log_add_fusion.12, pred[512,2048]{1,0:T(8,128)(4,1)} %get-tuple-element.1059), kind=kOutput, calls=%fused_computation.109.clone.1 | convolution fusion | flops 437259776 | bytes 27990016 | tf_op jit(solution)/shard_map/while/body/eval_jaxpr/hqk,qhd->khd/dot_general | solution.py:143
  695.2 23.5 %fusion.836 = bf16[512,3,64]{0,2,1:T(8,128)(2,1)S(1)} fusion(bf16[2048,3,64]{0,2,1:T(8,128)(2,1)S(1)} %bitcast.687, f32[3,512,2048]{2,1,0:T(8,128)} %fusion.834, f32[3,512,2048]{2,1,0:T(8,128)} %copy-done.2, f32[3,512]{1,0:T(4,128)S(1)} %log_add_fusion.13, pred[512,2048]{1,0:T(8,128)(4,1)} %copy-done.8), kind=kOutput, calls=%fused_computation.248.clone.1 | convolution fusion | flops 437358080 | bytes 27203584 | tf_op jit(solution)/shard_map/while/body/eval_jaxpr/hqk,khd->qhd/dot_general | solution.py:141
  718.7 23.9 %fusion.837 = bf16[512,3,64]{0,2,1:T(8,128)(2,1)} fusion(bf16[2048,3,64]{0,2,1:T(8,128)(2,1)S(1)} %bitcast.688, f32[3,512,2048]{2,1,0:T(8,128)} %fusion.832, f32[3,512,2048]{2,1,0:T(8,128)} %copy-done.3, f32[3,512]{1,0:T(4,128)} %log_add_fusion.10, pred[512,2048]{1,0:T(8,128)(4,1)} %get-tuple-element.1049), kind=kOutput, calls=%fused_computation.247.clone.1 | convolution fusion | flops 437358080 | bytes 27203584 | tf_op jit(solution)/shard_map/while/body/eval_jaxpr/hqk,khd->qhd/dot_general | solution.py:141
  742.6 23.6 %fusion.838 = bf16[512,3,64]{0,2,1:T(8,128)(2,1)} fusion(bf16[2048,3,64]{0,2,1:T(8,128)(2,1)S(1)} %bitcast.689, f32[3,512,2048]{2,1,0:T(8,128)} %fusion.830, f32[3,512,2048]{2,1,0:T(8,128)} %copy-done.4, f32[3,512]{1,0:T(4,128)} %log_add_fusion.11, pred[512,2048]{1,0:T(8,128)(4,1)} %get-tuple-element.1056), kind=kOutput, calls=%fused_computation.246.clone.1 | convolution fusion | flops 437358080 | bytes 27203584 | tf_op jit(solution)/shard_map/while/body/eval_jaxpr/hqk,khd->qhd/dot_general | solution.py:141
  766.3 25.6 %fusion.831 = f32[3,64,2048]{2,1,0:T(8,128)} fusion(f32[3,64,2048]{2,1,0:T(8,128)} %fusion.829, bf16[512,3,64]{0,2,1:T(8,128)(2,1)S(1)} %bitcast.710, f32[3,512,2048]{2,1,0:T(8,128)} %fusion.830, f32[3,512,2048]{2,1,0:T(8,128)} %copy-done.4, f32[3,512]{1,0:T(4,128)} %log_add_fusion.11, pred[512,2048]{1,0:T(8,128)(4,1)} %get-tuple-element.1056), kind=kOutput, calls=%fused_computation.196.clone.1 | convolution fusion | flops 437652992 | bytes 29562880 | tf_op jit(solution)/shard_map/while/body/eval_jaxpr/hqk,qhd->khd/dot_general | solution.py:143
  791.9 26.3 %fusion.833 = f32[3,64,2048]{2,1,0:T(8,128)} fusion(f32[3,64,2048]{2,1,0:T(8,128)} %fusion.831, bf16[512,3,64]{0,2,1:T(8,128)(2,1)S(1)} %bitcast.708, f32[3,512,2048]{2,1,0:T(8,128)} %fusion.832, f32[3,512,2048]{2,1,0:T(8,128)} %copy-done.3, f32[3,512]{1,0:T(4,128)} %log_add_fusion.10, pred[512,2048]{1,0:T(8,128)(4,1)} %get-tuple-element.1049), kind=kOutput, calls=%fused_computation.195.clone.1 | convolution fusion | flops 437652992 | bytes 29562880 | tf_op jit(solution)/shard_map/while/body/eval_jaxpr/hqk,qhd->khd/dot_general | solution.py:143
  818.3 25.8 %fusion.835 = bf16[3,64,2048]{2,1,0:T(8,128)(2,1)} fusion(f32[3,64,2048]{2,1,0:T(8,128)} %fusion.833, bf16[512,3,64]{0,2,1:T(8,128)(2,1)S(1)} %bitcast.706, f32[3,512,2048]{2,1,0:T(8,128)} %fusion.834, f32[3,512,2048]{2,1,0:T(8,128)} %copy-done.2, f32[3,512]{1,0:T(4,128)S(1)} %log_add_fusion.13, pred[512,2048]{1,0:T(8,128)(4,1)} %copy-done.8), kind=kOutput, calls=%fused_computation.198.clone.1 | convolution fusion | flops 438046208 | bytes 28776448 | tf_op jit(solution)/shard_map/while/body/eval_jaxpr/hqk,qhd->khd/dot_general | solution.py:143
  901.6 23.6 %all-gather.5.cloned.1.call-done = bf16[2048,768]{1,0:T(8,128)(2,1)} async-done(((bf16[512,768]{1,0:T(8,128)(2,1)}), bf16[2048,768]{1,0:T(8,128)(2,1)}) %all-gather.5.cloned.1.call-update) | async-done | bytes 3145744 | tf_op jit(solution)/shard_map/while/body/eval_jaxpr/all_gather | solution.py:29
  977.2 37.9 %reduce-scatter.41.cloned.1.call-done = bf16[512,768]{1,0:T(8,128)(2,1)} async-done(((bf16[2048,768]{1,0:T(8,128)(2,1)}), bf16[512,768]{1,0:T(8,128)(2,1)}) %reduce-scatter.41.cloned.1.call-update) | async-done | bytes 786448 | tf_op jit(solution)/shard_map/while/body/eval_jaxpr/reduce_scatter | solution.py:41
  1019.0 28.6 %all-gather.7.cloned.1.call-done = bf16[2048,768]{1,0:T(8,128)(2,1)} async-done(((bf16[512,768]{1,0:T(8,128)(2,1)}), bf16[2048,768]{1,0:T(8,128)(2,1)}) %all-gather.7.cloned.1.call-update) | async-done | bytes 3145744 | tf_op jit(solution)/shard_map/while/body/eval_jaxpr/all_gather | solution.py:29
  1060.5 38.1 %reduce-scatter.43.cloned.1.call-done = bf16[512,768]{1,0:T(8,128)(2,1)} async-done(((bf16[2048,768]{1,0:T(8,128)(2,1)}), bf16[512,768]{1,0:T(8,128)(2,1)}) %reduce-scatter.43.cloned.1.call-update) | async-done | bytes 786448 | tf_op jit(solution)/shard_map/while/body/eval_jaxpr/reduce_scatter | solution.py:41
  1105.9 28.6 %all-gather.9.cloned.1.call-done = bf16[2048,768]{1,0:T(8,128)(2,1)} async-done(((bf16[512,768]{1,0:T(8,128)(2,1)}), bf16[2048,768]{1,0:T(8,128)(2,1)}) %all-gather.9.cloned.1.call-update) | async-done | bytes 3145744 | tf_op jit(solution)/shard_map/while/body/eval_jaxpr/all_gather | solution.py:35
  1149.1 37.7 %reduce-scatter.45.cloned.1.call-done = bf16[512,768]{1,0:T(8,128)(2,1)} async-done(((bf16[2048,768]{1,0:T(8,128)(2,1)}), bf16[512,768]{1,0:T(8,128)(2,1)}) %reduce-scatter.45.cloned.1.call-update) | async-done | bytes 786448 | tf_op jit(solution)/shard_map/while/body/eval_jaxpr/reduce_scatter | solution.py:50
  1195.2 26.8 %all-gather.11.cloned.1.call-done = bf16[2048,768]{1,0:T(8,128)(2,1)} async-done(((bf16[512,768]{1,0:T(8,128)(2,1)}), bf16[2048,768]{1,0:T(8,128)(2,1)}) %all-gather.11.cloned.1.call-update) | async-done | bytes 3145744 | tf_op jit(solution)/shard_map/while/body/eval_jaxpr/all_gather | solution.py:35
  1232.2 24.2 %fusion.839 = bf16[512,3,64]{0,2,1:T(8,128)(2,1)} fusion(bf16[2048,3,64]{0,2,1:T(8,128)(2,1)} %bitcast.686, f32[3,512,2048]{2,1,0:T(8,128)} %fusion.828, f32[3,512,2048]{2,1,0:T(8,128)} %copy-done.5, f32[3,512]{1,0:T(4,128)} %log_add_fusion.12, pred[512,2048]{1,0:T(8,128)(4,1)} %get-tuple-element.1059), kind=kOutput, calls=%fused_computation.245.clone.1 | convolution fusion | flops 437358080 | bytes 27203584 | tf_op jit(solution)/shard_map/while/body/eval_jaxpr/hqk,khd->qhd/dot_general | solution.py:141
  1256.4 27.7 %fusion.829 = f32[3,64,2048]{2,1,0:T(8,128)} fusion(bf16[512,3,64]{0,2,1:T(8,128)(2,1)} %bitcast.711, f32[3,512,2048]{2,1,0:T(8,128)} %fusion.828, f32[3,512,2048]{2,1,0:T(8,128)} %copy-done.5, f32[3,512]{1,0:T(4,128)} %log_add_fusion.12, pred[512,2048]{1,0:T(8,128)(4,1)} %get-tuple-element.1059), kind=kOutput, calls=%fused_computation.109.clone.1 | convolution fusion | flops 437259776 | bytes 27990016 | tf_op jit(solution)/shard_map/while/body/eval_jaxpr/hqk,qhd->khd/dot_general | solution.py:143
  1326.7 23.5 %fusion.836 = bf16[512,3,64]{0,2,1:T(8,128)(2,1)S(1)} fusion(bf16[2048,3,64]{0,2,1:T(8,128)(2,1)S(1)} %bitcast.687, f32[3,512,2048]{2,1,0:T(8,128)} %fusion.834, f32[3,512,2048]{2,1,0:T(8,128)} %copy-done.2, f32[3,512]{1,0:T(4,128)S(1)} %log_add_fusion.13, pred[512,2048]{1,0:T(8,128)(4,1)} %copy-done.8), kind=kOutput, calls=%fused_computation.248.clone.1 | convolution fusion | flops 437358080 | bytes 27203584 | tf_op jit(solution)/shard_map/while/body/eval_jaxpr/hqk,khd->qhd/dot_general | solution.py:141
  1350.2 23.9 %fusion.837 = bf16[512,3,64]{0,2,1:T(8,128)(2,1)} fusion(bf16[2048,3,64]{0,2,1:T(8,128)(2,1)S(1)} %bitcast.688, f32[3,512,2048]{2,1,0:T(8,128)} %fusion.832, f32[3,512,2048]{2,1,0:T(8,128)} %copy-done.3, f32[3,512]{1,0:T(4,128)} %log_add_fusion.10, pred[512,2048]{1,0:T(8,128)(4,1)} %get-tuple-element.1049), kind=kOutput, calls=%fused_computation.247.clone.1 | convolution fusion | flops 437358080 | bytes 27203584 | tf_op jit(solution)/shard_map/while/body/eval_jaxpr/hqk,khd->qhd/dot_general | solution.py:141
  1374.2 23.6 %fusion.838 = bf16[512,3,64]{0,2,1:T(8,128)(2,1)} fusion(bf16[2048,3,64]{0,2,1:T(8,128)(2,1)S(1)} %bitcast.689, f32[3,512,2048]{2,1,0:T(8,128)} %fusion.830, f32[3,512,2048]{2,1,0:T(8,128)} %copy-done.4, f32[3,512]{1,0:T(4,128)} %log_add_fusion.11, pred[512,2048]{1,0:T(8,128)(4,1)} %get-tuple-element.1056), kind=kOutput, calls=%fused_computation.246.clone.1 | convolution fusion | flops 437358080 | bytes 27203584 | tf_op jit(solution)/shard_map/while/body/eval_jaxpr/hqk,khd->qhd/dot_general | solution.py:141
  1397.8 25.6 %fusion.831 = f32[3,64,2048]{2,1,0:T(8,128)} fusion(f32[3,64,2048]{2,1,0:T(8,128)} %fusion.829, bf16[512,3,64]{0,2,1:T(8,128)(2,1)S(1)} %bitcast.710, f32[3,512,2048]{2,1,0:T(8,128)} %fusion.830, f32[3,512,2048]{2,1,0:T(8,128)} %copy-done.4, f32[3,512]{1,0:T(4,128)} %log_add_fusion.11, pred[512,2048]{1,0:T(8,128)(4,1)} %get-tuple-element.1056), kind=kOutput, calls=%fused_computation.196.clone.1 | convolution fusion | flops 437652992 | bytes 29562880 | tf_op jit(solution)/shard_map/while/body/eval_jaxpr/hqk,qhd->khd/dot_general | solution.py:143
  1423.5 26.3 %fusion.833 = f32[3,64,2048]{2,1,0:T(8,128)} fusion(f32[3,64,2048]{2,1,0:T(8,128)} %fusion.831, bf16[512,3,64]{0,2,1:T(8,128)(2,1)S(1)} %bitcast.708, f32[3,512,2048]{2,1,0:T(8,128)} %fusion.832, f32[3,512,2048]{2,1,0:T(8,128)} %copy-done.3, f32[3,512]{1,0:T(4,128)} %log_add_fusion.10, pred[512,2048]{1,0:T(8,128)(4,1)} %get-tuple-element.1049), kind=kOutput, calls=%fused_computation.195.clone.1 | convolution fusion | flops 437652992 | bytes 29562880 | tf_op jit(solution)/shard_map/while/body/eval_jaxpr/hqk,qhd->khd/dot_general | solution.py:143
  1449.8 25.8 %fusion.835 = bf16[3,64,2048]{2,1,0:T(8,128)(2,1)} fusion(f32[3,64,2048]{2,1,0:T(8,128)} %fusion.833, bf16[512,3,64]{0,2,1:T(8,128)(2,1)S(1)} %bitcast.706, f32[3,512,2048]{2,1,0:T(8,128)} %fusion.834, f32[3,512,2048]{2,1,0:T(8,128)} %copy-done.2, f32[3,512]{1,0:T(4,128)S(1)} %log_add_fusion.13, pred[512,2048]{1,0:T(8,128)(4,1)} %copy-done.8), kind=kOutput, calls=%fused_computation.198.clone.1 | convolution fusion | flops 438046208 | bytes 28776448 | tf_op jit(solution)/shard_map/while/body/eval_jaxpr/hqk,qhd->khd/dot_general | solution.py:143
  1536.6 37.0 %collective-permute-done.1 = bf16[2,512,768]{2,1,0:T(8,128)(2,1)} collective-permute-done((bf16[2,512,768]{2,1,0:T(8,128)(2,1)}, bf16[2,512,768]{2,1,0:T(8,128)(2,1)}, u32[]{:S(2)}, u32[]{:S(2)}) %collective-permute-start.1) | collective-permute-done | bytes 1572896 | tf_op jit(solution)/shard_map/ppermute | solution.py:21
  1575.5 358.4 %while.60 = (s32[]{:T(128)}, f32[3,768,192]{1,2,0:T(8,128)}, f32[192,768]{1,0:T(8,128)}, f32[768,768]{1,0:T(8,128)}, f32[768,768]{1,0:T(8,128)}, /*index=5*/f32[...) while((s32[]{:T(128)}, f32[3,768,192]{1,2,0:T(8,128)}, ...), condition=%wide.region_53.54_spmd.clone, body=%wide.region_36.53_spmd.clone.sunk | while | flops 3497013248 | bytes 68125344 | solution.py:409
  1682.9 23.2 %reduce-scatter.57.cloned.1.call-done = bf16[64,768]{1,0:T(8,128)(2,1)} async-done(((bf16[256,768]{1,0:T(8,128)(2,1)}), bf16[64,768]{1,0:T(8,128)(2,1)}) %reduce-scatter.57.cloned.1.call-update) | async-done | bytes 98320 | tf_op jit(solution)/shard_map/while/body/eval_jaxpr/reduce_scatter | solution.py:41
  1724.4 18.4 reduce-scatter.59.cloned.1.call-done
  1761.7 18.6 reduce-scatter.49.cloned.1.call-done
  1862.8 23.2 %reduce-scatter.57.cloned.1.call-done = bf16[64,768]{1,0:T(8,128)(2,1)} async-done(((bf16[256,768]{1,0:T(8,128)(2,1)}), bf16[64,768]{1,0:T(8,128)(2,1)}) %reduce-scatter.57.cloned.1.call-update) | async-done | bytes 98320 | tf_op jit(solution)/shard_map/while/body/eval_jaxpr/reduce_scatter | solution.py:41
  1980.3 27.8 %reduce-scatter.25.cloned.1.call-done = bf16[3,192,192]{2,1,0:T(8,128)(2,1)} async-done(((bf16[3,768,192]{2,1,0:T(8,128)(2,1)}), bf16[3,192,192]{2,1,0:T(8,128)(2,1)}) %reduce-scatter.25.cloned.1.call-update) | async-done | bytes 221200 | tf_op jit(solution)/shard_map/reduce_scatter | solution.py:60
  2009.9 28.3 %reduce-scatter.31.cloned.1.call-done = bf16[192,768]{1,0:T(8,128)(2,1)} async-done(((bf16[768,768]{1,0:T(8,128)(2,1)}), bf16[192,768]{1,0:T(8,128)(2,1)}) %reduce-scatter.31.cloned.1.call-update) | async-done | bytes 294928
  2040.5 27.9 %reduce-scatter.27.cloned.1.call-done = bf16[192,768]{1,0:T(8,128)(2,1)} async-done(((bf16[768,768]{1,0:T(8,128)(2,1)}), bf16[192,768]{1,0:T(8,128)(2,1)}) %reduce-scatter.27.cloned.1.call-update) | async-done | bytes 294928 | tf_op jit(solution)/shard_map/reduce_scatter | solution.py:66
  (783 shorter events, 834.8 us)
Async XLA Ops:
  10.0 28.6 %reduce-scatter.35.cloned.1.call-start = ((), (), s32[]{:S(2)}) async-start(), calls=%async_computation.23 | async-start | bytes 491520 | tf_op jit(solution)/shard_map/while/body/eval_jaxpr/reduce_scatter | solution.py:263
  14.9 67.6 %copy-start.26 = (bf16[768,768]{1,0:T(8,128)(2,1)S(1)}, bf16[768,768]{1,0:T(8,128)(2,1)}, u32[]{:S(2)}) copy-start(bf16[768,768]{1,0:T(8,128)(2,1)} %get-tuple-element.1148) | copy-start | bytes 3538948 | tf_op jit(solution)/shard_map/while
  14.9 59.3 %reduce-scatter.37.cloned.1.call-start = ((), (), s32[]{:S(2)}) async-start(), calls=%async_computation.24 | async-start | bytes 491520 | tf_op jit(solution)/shard_map/while/body/eval_jaxpr/reduce_scatter | solution.py:41
  49.0 64.9 %copy-start.25 = (bf16[2,512,768]{2,1,0:T(8,128)(2,1)S(1)}, bf16[2,512,768]{2,1,0:T(8,128)(2,1)}, u32[]{:S(2)}) copy-start(bf16[2,512,768]{2,1,0:T(8,128)(2,1)} %get-tuple-element.1141) | copy-start | bytes 4718596 | tf_op jit(solution)/shard_map/while
  52.9 53.8 %reduce-scatter.39.cloned.1.call-start = ((), (), s32[]{:S(2)}) async-start(), calls=%async_computation.25 | async-start | bytes 491520 | tf_op jit(solution)/shard_map/while/body/eval_jaxpr/reduce_scatter | solution.py:41
  116.0 26.3 %reduce-scatter.35.cloned.1.call-start = ((), (), s32[]{:S(2)}) async-start(), calls=%async_computation.23 | async-start | bytes 491520 | tf_op jit(solution)/shard_map/while/body/eval_jaxpr/reduce_scatter | solution.py:263
  121.0 65.2 %copy-start.26 = (bf16[768,768]{1,0:T(8,128)(2,1)S(1)}, bf16[768,768]{1,0:T(8,128)(2,1)}, u32[]{:S(2)}) copy-start(bf16[768,768]{1,0:T(8,128)(2,1)} %get-tuple-element.1148) | copy-start | bytes 3538948 | tf_op jit(solution)/shard_map/while
  121.0 56.9 %reduce-scatter.37.cloned.1.call-start = ((), (), s32[]{:S(2)}) async-start(), calls=%async_computation.24 | async-start | bytes 491520 | tf_op jit(solution)/shard_map/while/body/eval_jaxpr/reduce_scatter | solution.py:41
  152.7 65.0 %copy-start.25 = (bf16[2,512,768]{2,1,0:T(8,128)(2,1)S(1)}, bf16[2,512,768]{2,1,0:T(8,128)(2,1)}, u32[]{:S(2)}) copy-start(bf16[2,512,768]{2,1,0:T(8,128)(2,1)} %get-tuple-element.1141) | copy-start | bytes 4718596 | tf_op jit(solution)/shard_map/while
  156.6 53.8 %reduce-scatter.39.cloned.1.call-start = ((), (), s32[]{:S(2)}) async-start(), calls=%async_computation.25 | async-start | bytes 491520 | tf_op jit(solution)/shard_map/while/body/eval_jaxpr/reduce_scatter | solution.py:41
  219.7 37.8 %collective-permute-start = (bf16[2,512,768]{2,1,0:T(8,128)(2,1)}, bf16[2,512,768]{2,1,0:T(8,128)(2,1)S(1)}, u32[]{:S(2)}, u32[]{:S(2)}) collective-permute-start(bf16[2,512,768]{2,1,0:T(8,128)(2,1)} %get-tuple-element.463), channel_id=1, source_target_pairs={{0,16},{1,17},{2,18},{3,19},{4,20},{5,21},{6,22},{7,23},{8,24},{9,... | collective-permute-start | bytes 4718600 | tf_op jit(solution)/shard_map/ppermute | solution.py:21
  260.9 32.7 %all-gather.5.cloned.1.call-start = ((), (), s32[]{:S(2)}) async-start(), calls=%async_computation.26 | async-start | bytes 3932160 | tf_op jit(solution)/shard_map/while/body/eval_jaxpr/all_gather | solution.py:29
  262.4 121.2 %reduce-scatter.41.cloned.1.call-start = ((), (), s32[]{:S(2)}) async-start(), calls=%async_computation.27 | async-start | bytes 3932160 | tf_op jit(solution)/shard_map/while/body/eval_jaxpr/reduce_scatter | solution.py:41
  345.4 70.6 %all-gather.7.cloned.1.call-start = ((), (), s32[]{:S(2)}) async-start(), calls=%async_computation.28 | async-start | bytes 3932160 | tf_op jit(solution)/shard_map/while/body/eval_jaxpr/all_gather | solution.py:29
  387.4 79.6 %reduce-scatter.43.cloned.1.call-start = ((), (), s32[]{:S(2)}) async-start(), calls=%async_computation.29 | async-start | bytes 3932160 | tf_op jit(solution)/shard_map/while/body/eval_jaxpr/reduce_scatter | solution.py:41
  428.9 74.1 %all-gather.9.cloned.1.call-start = ((), (), s32[]{:S(2)}) async-start(), calls=%async_computation.30 | async-start | bytes 3932160 | tf_op jit(solution)/shard_map/while/body/eval_jaxpr/all_gather | solution.py:35
  474.3 80.9 %reduce-scatter.45.cloned.1.call-start = ((), (), s32[]{:S(2)}) async-start(), calls=%async_computation.31 | async-start | bytes 3932160 | tf_op jit(solution)/shard_map/while/body/eval_jaxpr/reduce_scatter | solution.py:50
  517.1 73.3 %all-gather.11.cloned.1.call-start = ((), (), s32[]{:S(2)}) async-start(), calls=%async_computation.32 | async-start | bytes 3932160 | tf_op jit(solution)/shard_map/while/body/eval_jaxpr/all_gather | solution.py:35
  561.7 327.5 %reduce-scatter.47.cloned.1.call-start = ((), (), s32[]{:S(2)}) async-start(), calls=%async_computation.33 | async-start | bytes 3932160 | tf_op jit(solution)/shard_map/while/body/eval_jaxpr/reduce_scatter | solution.py:50
  894.0 31.2 %all-gather.5.cloned.1.call-start = ((), (), s32[]{:S(2)}) async-start(), calls=%async_computation.26 | async-start | bytes 3932160 | tf_op jit(solution)/shard_map/while/body/eval_jaxpr/all_gather | solution.py:29
  895.5 119.6 %reduce-scatter.41.cloned.1.call-start = ((), (), s32[]{:S(2)}) async-start(), calls=%async_computation.27 | async-start | bytes 3932160 | tf_op jit(solution)/shard_map/while/body/eval_jaxpr/reduce_scatter | solution.py:41
  977.0 70.6 %all-gather.7.cloned.1.call-start = ((), (), s32[]{:S(2)}) async-start(), calls=%async_computation.28 | async-start | bytes 3932160 | tf_op jit(solution)/shard_map/while/body/eval_jaxpr/all_gather | solution.py:29
  1018.9 79.6 %reduce-scatter.43.cloned.1.call-start = ((), (), s32[]{:S(2)}) async-start(), calls=%async_computation.29 | async-start | bytes 3932160 | tf_op jit(solution)/shard_map/while/body/eval_jaxpr/reduce_scatter | solution.py:41
  1060.4 74.1 %all-gather.9.cloned.1.call-start = ((), (), s32[]{:S(2)}) async-start(), calls=%async_computation.30 | async-start | bytes 3932160 | tf_op jit(solution)/shard_map/while/body/eval_jaxpr/all_gather | solution.py:35
  1105.9 80.9 %reduce-scatter.45.cloned.1.call-start = ((), (), s32[]{:S(2)}) async-start(), calls=%async_computation.31 | async-start | bytes 3932160 | tf_op jit(solution)/shard_map/while/body/eval_jaxpr/reduce_scatter | solution.py:50
  1148.7 73.3 %all-gather.11.cloned.1.call-start = ((), (), s32[]{:S(2)}) async-start(), calls=%async_computation.32 | async-start | bytes 3932160 | tf_op jit(solution)/shard_map/while/body/eval_jaxpr/all_gather | solution.py:35
  1193.3 327.5 %reduce-scatter.47.cloned.1.call-start = ((), (), s32[]{:S(2)}) async-start(), calls=%async_computation.33 | async-start | bytes 3932160 | tf_op jit(solution)/shard_map/while/body/eval_jaxpr/reduce_scatter | solution.py:50
  1535.3 38.4 %collective-permute-start.1 = (bf16[2,512,768]{2,1,0:T(8,128)(2,1)}, bf16[2,512,768]{2,1,0:T(8,128)(2,1)}, u32[]{:S(2)}, u32[]{:S(2)}) collective-permute-start(bf16[2,512,768]{2,1,0:T(8,128)(2,1)} %get-tuple-element.464), channel_id=1, source_target_pairs={{16,0},{17,1},{18,2},{19,3},{20,4},{21,5},{22,6},{23,7},{24,8},{25... | collective-permute-start | bytes 4718600 | tf_op jit(solution)/shard_map/ppermute | solution.py:21
  1575.5 358.5 %copy-start.62 = (f32[3,768]{1,0:T(4,128)S(1)}, f32[3,768]{1,0:T(4,128)}, u32[]{:S(2)}) copy-start(f32[3,768]{1,0:T(4,128)} %get-tuple-element.476) | copy-start | bytes 27652
  1575.5 25.0 %reduce-scatter.49.cloned.1.call-start = ((), (), s32[]{:S(2)}) async-start(), calls=%async_computation.34 | async-start | bytes 491520 | tf_op jit(solution)/shard_map/while/body/eval_jaxpr/reduce_scatter | solution.py:263
  1580.5 43.3 %reduce-scatter.51.cloned.1.call-start = ((), (), s32[]{:S(2)}) async-start(), calls=%async_computation.35 | async-start | bytes 491520 | tf_op jit(solution)/shard_map/while/body/eval_jaxpr/reduce_scatter | solution.py:299
  1582.9 64.7 %reduce-scatter.53.cloned.1.call-start = ((), (), s32[]{:S(2)}) async-start(), calls=%async_computation.36 | async-start | bytes 491520 | tf_op jit(solution)/shard_map/while/body/eval_jaxpr/reduce_scatter | solution.py:41
  1612.3 70.6 %reduce-scatter.55.cloned.1.call-start = ((), (), s32[]{:S(2)}) async-start(), calls=%async_computation.37 | async-start | bytes 491520 | tf_op jit(solution)/shard_map/while/body/eval_jaxpr/reduce_scatter | solution.py:50
  1661.6 44.5 %reduce-scatter.57.cloned.1.call-start = ((), (), s32[]{:S(2)}) async-start(), calls=%async_computation.38 | async-start | bytes 491520 | tf_op jit(solution)/shard_map/while/body/eval_jaxpr/reduce_scatter | solution.py:41
  1664.6 78.2 %reduce-scatter.59.cloned.1.call-start = ((), (), s32[]{:S(2)}) async-start(), calls=%async_computation.39 | async-start | bytes 491520 | tf_op jit(solution)/shard_map/while/body/eval_jaxpr/reduce_scatter | solution.py:50
  1666.6 53.6 %copy-start.16 = (bf16[3,768,192]{1,2,0:T(8,128)(2,1)S(1)}, bf16[3,768,192]{1,2,0:T(8,128)(2,1)}, u32[]{:S(2)}) copy-start(bf16[3,768,192]{1,2,0:T(8,128)(2,1)} %get-tuple-element.1256) | copy-start | bytes 2654212 | tf_op jit(solution)/shard_map/while
  1754.1 26.3 %reduce-scatter.49.cloned.1.call-start = ((), (), s32[]{:S(2)}) async-start(), calls=%async_computation.34 | async-start | bytes 491520 | tf_op jit(solution)/shard_map/while/body/eval_jaxpr/reduce_scatter | solution.py:263
  1759.1 44.5 %reduce-scatter.51.cloned.1.call-start = ((), (), s32[]{:S(2)}) async-start(), calls=%async_computation.35 | async-start | bytes 491520 | tf_op jit(solution)/shard_map/while/body/eval_jaxpr/reduce_scatter | solution.py:299
  1761.5 66.0 %reduce-scatter.53.cloned.1.call-start = ((), (), s32[]{:S(2)}) async-start(), calls=%async_computation.36 | async-start | bytes 491520 | tf_op jit(solution)/shard_map/while/body/eval_jaxpr/reduce_scatter | solution.py:41
  1792.1 70.6 %reduce-scatter.55.cloned.1.call-start = ((), (), s32[]{:S(2)}) async-start(), calls=%async_computation.37 | async-start | bytes 491520 | tf_op jit(solution)/shard_map/while/body/eval_jaxpr/reduce_scatter | solution.py:50
  1841.5 44.5 %reduce-scatter.57.cloned.1.call-start = ((), (), s32[]{:S(2)}) async-start(), calls=%async_computation.38 | async-start | bytes 491520 | tf_op jit(solution)/shard_map/while/body/eval_jaxpr/reduce_scatter | solution.py:41
  1844.5 78.3 %reduce-scatter.59.cloned.1.call-start = ((), (), s32[]{:S(2)}) async-start(), calls=%async_computation.39 | async-start | bytes 491520 | tf_op jit(solution)/shard_map/while/body/eval_jaxpr/reduce_scatter | solution.py:50
  1848.1 52.0 %copy-start.16 = (bf16[3,768,192]{1,2,0:T(8,128)(2,1)S(1)}, bf16[3,768,192]{1,2,0:T(8,128)(2,1)}, u32[]{:S(2)}) copy-start(bf16[3,768,192]{1,2,0:T(8,128)(2,1)} %get-tuple-element.1256) | copy-start | bytes 2654212 | tf_op jit(solution)/shard_map/while
  1933.9 23.0 %reduce-scatter.33.cloned.1.call-start = ((), (), s32[]{:S(2)}) async-start(), calls=%async_computation.22 | async-start | bytes 245760
  1934.9 43.7 %reduce-scatter.29.cloned.1.call-start = ((), (), s32[]{:S(2)}) async-start(), calls=%async_computation.20 | async-start | bytes 491520
  1937.0 71.0 %reduce-scatter.25.cloned.1.call-start = ((), (), s32[]{:S(2)}) async-start(), calls=%async_computation.18 | async-start | bytes 1474560 | tf_op jit(solution)/shard_map/reduce_scatter | solution.py:60
  1942.9 95.3 %reduce-scatter.31.cloned.1.call-start = ((), (), s32[]{:S(2)}) async-start(), calls=%async_computation.21 | async-start | bytes 1474560
  1946.3 122.0 %reduce-scatter.27.cloned.1.call-start = ((), (), s32[]{:S(2)}) async-start(), calls=%async_computation.19 | async-start | bytes 1474560 | tf_op jit(solution)/shard_map/reduce_scatter | solution.py:66
  (168 other events, 2292.0 us)
Sparse Core Ops, SparseCore 0:
  15.0 23.5 reduce-scatter.34
  53.1 21.1 reduce-scatter.36
  85.6 21.1 reduce-scatter.38
  121.1 21.1 reduce-scatter.34
  156.8 21.1 reduce-scatter.36
  189.3 21.1 reduce-scatter.38
  263.9 29.7 all-gather.4
  345.6 37.9 reduce-scatter.40
  387.5 28.5 all-gather.6
  429.0 37.9 reduce-scatter.42
  474.4 28.5 all-gather.8
  517.2 37.9 reduce-scatter.44
  561.9 28.5 all-gather.10
  851.2 37.9 reduce-scatter.46
  896.6 28.4 all-gather.4
  977.1 37.9 reduce-scatter.40
  1019.0 28.5 all-gather.6
  1060.6 37.9 reduce-scatter.42
  1106.0 28.5 all-gather.8
  1148.8 37.9 reduce-scatter.44
  1193.4 28.5 all-gather.10
  1482.8 37.9 reduce-scatter.46
  1580.6 19.8 reduce-scatter.48
  1602.9 20.7 reduce-scatter.50
  1626.8 20.7 reduce-scatter.52
  1661.7 21.1 reduce-scatter.54
  1685.2 20.8 reduce-scatter.56
  1721.7 21.1 reduce-scatter.58
  1759.2 21.1 reduce-scatter.48
  1782.7 20.8 reduce-scatter.50
  1806.7 20.8 reduce-scatter.52
  1841.6 21.1 reduce-scatter.54
  1865.1 20.8 reduce-scatter.56
  1901.5 21.1 reduce-scatter.58
Sparse Core Ops, SparseCore 1:
  1937.2 19.7 reduce-scatter.32
  1959.8 18.8 reduce-scatter.28
  1980.8 27.2 reduce-scatter.24
  2010.4 27.8 reduce-scatter.30
  2040.5 27.8 reduce-scatter.26
where the time goes:
time: 2090 us; the launch traced here: 2080 us
  waiting for transfers between devices  971 us (46%)
  matrix products  778 us (37%)
  other arithmetic  142 us (7%)
  blocking collectives  104 us (5%)
  local copies, waits for them, and re-layouts  46.1 us (2%)
    reduce_scatter x12, waiting for transfers between devices, gather_sums(): lax.psum_scatter(term(jnp.int32(0), row_count * lax.axis_size('tensor'))....  311 us
    dot_general x10, matrix products, attention_backward(): jnp.einsum('hqk,qhd->khd', score_grad, query_block, preferred_element_typ...  215 us
    dot_general x10, matrix products, attention_backward(): jnp.einsum('hqk,khd->qhd', score_grad, keys_all, preferred_element_type=j...  195 us
    reduce_scatter x8, waiting for transfers between devices, gather_grad_sums(): lax.psum_scatter(term(jnp.int32(0), row_count * lax.axis_size('tensor'))....  164 us
    all_gather x4, waiting for transfers between devices, spread_grads(): lax.all_gather(as_sent(values), 'tensor', axis=0, tiled=True)  111 us
    all_gather x4, waiting for transfers between devices, spread_rows(): return lax.all_gather(values, 'tensor', axis=0, tiled=True)  106 us
    reduce_scatter x4, waiting for transfers between devices, routed_forward(): lax.psum_scatter(pick_term(jnp.int32(0), pick_count * lax.axis_size('tens...  80.5 us
    ppermute x2, waiting for transfers between devices, passed_along(): return lax.ppermute(block, axis, route)  71.3 us
  transfers between devices with their start and end apart: 41, of which 41 were waited for; matrix products, arithmetic and copies ran while one was open for 6% of the time, Pallas kernels for 0%

commit v1 on v0

v1 whole, which is shorter than its diff:
```python
import functools

import jax
import jax.numpy as jnp
from jax import lax
from jax.experimental import pallas as pl
from jax.experimental.pallas import tpu as pltpu
from jax.sharding import PartitionSpec as P

HEADS = 12
EPSILON = 1e-06
NEGATIVE = -1e30
BF = jnp.bfloat16
F32 = jnp.float32
PAD = 256
MIB = 1 << 20


def swap(block, axis, bit):
    count = lax.axis_size(axis)
    return lax.ppermute(block, axis, [(i, i ^ bit) for i in range(count)])


def hop(block, source, target):
    return lax.ppermute(block, "section", [(source, target)])


def dot(left, right):
    return lax.dot_general(left, right, (((1,), (0,)), ((), ())), preferred_element_type=F32)


def dot_nt(left, right):
    return lax.dot_general(left, right, (((1,), (1,)), ((), ())), preferred_element_type=F32)


def dot_tn(left, right):
    return lax.dot_general(left, right, (((0,), (0,)), ((), ())), preferred_element_type=F32)


def unit_rows(values):
    scale = lax.rsqrt(jnp.mean(values * values, axis=-1, keepdims=True) + EPSILON)
    return values * scale, scale


def norm_back(unit, scale, gain, grad):
    e = grad * gain
    return scale * (e - unit * jnp.mean(e * unit, axis=-1, keepdims=True))


def gelu_pair(x):
    c = 0.7978845608028654
    a = 0.044715
    xx = x * x
    th = jnp.tanh(c * (x + a * (x * xx)))
    half = 0.5 * (1.0 + th)
    slope = half + (0.5 * x) * (1.0 - th * th) * (c * (1.0 + (3.0 * a) * xx))
    return x * half, slope


def lanes(rows, width):
    return lax.broadcasted_iota(jnp.int32, (rows, width), 1)


def subs(rows, width):
    return lax.broadcasted_iota(jnp.int32, (rows, width), 0)


def head_of(values, lane, head, width):
    zero = jnp.zeros_like(values)
    return jnp.where((lane >= head * width) & (lane < (head + 1) * width), values, zero)


def three_pieces(column):
    first = column.astype(BF)
    rest = column - first.astype(F32)
    second = rest.astype(BF)
    third = (rest - second.astype(F32)).astype(BF)
    return first, second, third


def params(limit=56, grid=None):
    if grid is None:
        return pltpu.CompilerParams(vmem_limit_bytes=limit * MIB)
    return pltpu.CompilerParams(
        vmem_limit_bytes=limit * MIB, dimension_semantics=("arbitrary",) * grid
    )


VM = pl.BlockSpec(memory_space=pltpu.VMEM)
SM = pl.BlockSpec(memory_space=pltpu.SMEM)
HB = pl.BlockSpec(memory_space=pl.ANY)


def shape(dims, dtype):
    return jax.ShapeDtypeStruct(dims, dtype)


def halves_out(partial, low, keep_ref, send_ref):
    pick = partial.shape[0] // 2
    half = pick // 2
    for s in range(2):
        first = partial[s * pick : s * pick + half]
        second = partial[s * pick + half : (s + 1) * pick]
        keep_ref[s] = jnp.where(low == 0, first, second).astype(BF)
        send_ref[s] = jnp.where(low == 0, second, first).astype(BF)


def halves_in(own_ref, other_ref, low):
    parts = []
    for s in range(2):
        own, other = own_ref[s].astype(F32), other_ref[s].astype(F32)
        parts.append(jnp.where(low == 0, own, other))
        parts.append(jnp.where(low == 0, other, own))
    return jnp.concatenate(parts, 0)


def pick_kernel(info, rows_ref, sel_ref, keep_ref, send_ref):
    tensor, low = info[0], info[2]
    own = rows_ref.shape[1]
    pick = sel_ref.shape[1]
    parts = []
    for s in range(2):
        table = (sel_ref[s] == lanes(pick, own) + tensor * own).astype(F32).astype(BF)
        parts.append(dot(table, rows_ref[s]))
    halves_out(jnp.concatenate(parts, 0), low, keep_ref, send_ref)


def pick_rows(info, rows, sel_col):
    _, _, d = rows.shape
    pick = sel_col.shape[1]
    out = shape((2, pick // 2, d), BF)
    return pl.pallas_call(
        pick_kernel,
        out_shape=(out, out),
        in_specs=[SM, VM, VM],
        out_specs=(VM, VM),
        compiler_params=params(),
        name="pick",
    )(info, rows, sel_col)


def routed_attn_kernel(
    heads, info, own_ref, other_ref, gains_ref, qkv_ref, mix_ref,
    picked_ref, normed_ref, q_ref, k_ref, v_ref, mixed_ref, keep_ref, send_ref,
):
    low = info[2]
    picked = halves_in(own_ref, other_ref, low)
    picked_ref[...] = picked.astype(BF)
    unit, _ = unit_rows(picked)
    normed = (unit * gains_ref[0:1, :]).astype(BF)
    normed_ref[...] = normed
    width = qkv_ref.shape[2] // heads
    q = dot(normed, qkv_ref[0]).astype(BF)
    k = dot(normed, qkv_ref[1]).astype(BF)
    v = dot(normed, qkv_ref[2]).astype(BF)
    q = (q.astype(F32) * width ** (-0.5)).astype(BF)
    q_ref[...] = q
    k_ref[...] = k
    v_ref[...] = v
    pick = picked.shape[0] // 2
    lane = lanes(pick, heads * width)
    allowed = lanes(pick, pick) <= subs(pick, pick)
    parts = []
    for s in range(2):
        span = slice(s * pick, (s + 1) * pick)
        total = jnp.zeros((pick, heads * width), F32)
        for h in range(heads):
            scores = dot_nt(head_of(q[span], lane, h, width), k[span])
            scores = jnp.where(allowed, scores, NEGATIVE)
            expos = jnp.exp(scores - jnp.max(scores, axis=-1, keepdims=True))
            probs = expos / jnp.sum(expos, axis=-1, keepdims=True)
            total = total + dot(probs.astype(BF), head_of(v[span], lane, h, width))
        parts.append(total.astype(BF))
    mixed = jnp.concatenate(parts, 0)
    mixed_ref[...] = mixed
    halves_out(dot(mixed, mix_ref[...]), low, keep_ref, send_ref)


def routed_attn(info, own, other, gains, qkv_w, mix_w, heads):
    _, half, d = own.shape
    rows = 4 * half
    cols = qkv_w.shape[2]
    part = shape((2, half, d), BF)
    wide, narrow = shape((rows, d), BF), shape((rows, cols), BF)
    return pl.pallas_call(
        functools.partial(routed_attn_kernel, heads),
        out_shape=(wide, wide, narrow, narrow, narrow, narrow, part, part),
        in_specs=[SM] + [VM] * 5,
        out_specs=(VM,) * 8,
        compiler_params=params(),
        name="routed_attn",
    )(info, own, other, gains, qkv_w, mix_w)


def routed_mlp_kernel(
    info, picked_ref, own_ref, other_ref, gains_ref, up_ref, down_ref,
    attn_ref, normed_ref, act_ref, slope_ref, keep_ref, send_ref,
):
    low = info[2]
    attn = halves_in(own_ref, other_ref, low)
    attn_ref[...] = attn.astype(BF)
    unit, _ = unit_rows(picked_ref[...].astype(F32) + attn)
    normed = (unit * gains_ref[1:2, :]).astype(BF)
    normed_ref[...] = normed
    act, slope = gelu_pair(dot(normed, up_ref[...]))
    act = act.astype(BF)
    act_ref[...] = act
    slope_ref[...] = slope
    halves_out(dot(act, down_ref[...]), low, keep_ref, send_ref)


def routed_mlp(info, picked, own, other, gains, up_w, down_w):
    rows, d = picked.shape
    hidden = up_w.shape[1]
    part = shape((2, rows // 4, d), BF)
    return pl.pallas_call(
        routed_mlp_kernel,
        out_shape=(
            shape((rows, d), BF), shape((rows, d), BF), shape((rows, hidden), BF),
            shape((rows, hidden), F32), part, part,
        ),
        in_specs=[SM] + [VM] * 6,
        out_specs=(VM,) * 6,
        compiler_params=params(),
        name="routed_mlp",
    )(info, picked, own, other, gains, up_w, down_w)


def update_kernel(picked_ref, attn_ref, mlp_ref, mlp2_ref, gains_ref, both_ref, update_ref):
    d = picked_ref.shape[2]
    weight = gains_ref[2:3, :] * d ** (-0.5)
    for s in range(2):
        router = jnp.sum(picked_ref[s].astype(F32) * weight, axis=-1, keepdims=True)
        both = attn_ref[s].astype(F32) + (mlp_ref[s].astype(F32) + mlp2_ref[s].astype(F32))
        both_ref[s] = both.astype(BF)
        update_ref[s] = (router * both).astype(BF)


def make_update(picked_half, attn_half, mlp_half, mlp_far, gains):
    out = shape(picked_half.shape, BF)
    return pl.pallas_call(
        update_kernel,
        out_shape=(out, out),
        in_specs=[VM] * 5,
        out_specs=(VM, VM),
        compiler_params=params(),
        name="update",
    )(picked_half, attn_half, mlp_half, mlp_far, gains)


def routed_back_mlp_kernel(
    info, sel_own, sel_other, picked_ref, attn_ref, gains_ref, slope_ref, up_ref, down_ref,
    d_sel_ref, d_mlp_ref, d_pre_ref, gain_ref, keep_ref, send_ref,
):
    low = info[2]
    d = picked_ref.shape[1]
    d_sel = halves_in(sel_own, sel_other, low)
    d_sel_ref[...] = d_sel
    picked = picked_ref[...].astype(F32)
    router = jnp.sum(picked * (gains_ref[2:3, :] * d ** (-0.5)), axis=-1, keepdims=True)
    d_mlp = (router * d_sel).astype(BF)
    d_mlp_ref[...] = d_mlp
    d_pre = (dot_nt(d_mlp, down_ref[...]) * slope_ref[...]).astype(BF)
    d_pre_ref[...] = d_pre
    d_normed = dot_nt(d_pre, up_ref[...])
    unit, _ = unit_rows(picked + attn_ref[...].astype(F32))
    gain_ref[...] = jnp.sum(d_normed * unit, axis=0, keepdims=True)
    halves_out(d_normed, low, keep_ref, send_ref)


def routed_back_mlp(info, sel_own, sel_other, picked, attn, gains, slope, up_w, down_w):
    rows, d = picked.shape
    hidden = up_w.shape[1]
    part = shape((2, rows // 4, d), BF)
    return pl.pallas_call(
        routed_back_mlp_kernel,
        out_shape=(
            shape((rows, d), F32), shape((rows, d), BF), shape((rows, hidden), BF),
            shape((1, d), F32), part, part,
        ),
        in_specs=[SM] + [VM] * 8,
        out_specs=(VM,) * 6,
        compiler_params=params(),
        name="routed_back_mlp",
    )(info, sel_own, sel_other, picked, attn, gains, slope, up_w, down_w)


def routed_back_attn_kernel(
    heads, info, own_ref, other_ref, d_sel_ref, picked_ref, attn_ref, both_own, both_other,
    gains_ref, q_ref, k_ref, v_ref, qkv_ref, mix_ref,
    d_mid_ref, d_low_ref, d_qkv_ref, vec_ref, keep_ref, send_ref,
):
    low = info[2]
    rows, d = picked_ref.shape
    d_normed2 = halves_in(own_ref, other_ref, low)
    picked = picked_ref[...].astype(F32)
    d_sel = d_sel_ref[...]
    router_row = gains_ref[2:3, :] * d ** (-0.5)
    router = jnp.sum(picked * router_row, axis=-1, keepdims=True)
    unit2, scale2 = unit_rows(picked + attn_ref[...].astype(F32))
    d_mid = norm_back(unit2, scale2, gains_ref[1:2, :], d_normed2)
    both = halves_in(both_own, both_other, low)
    d_router = jnp.sum(d_sel * both, axis=-1, keepdims=True)
    d_mid_ref[...] = d_mid + d_router * router_row
    d_weight = jnp.sum(picked * d_router, axis=0, keepdims=True) * d ** (-0.5)
    vec_ref[1:2, :] = jnp.where(info[0] == 0, d_weight, jnp.zeros_like(d_weight))
    d_low = (router * d_sel + d_mid).astype(BF)
    d_low_ref[...] = d_low
    d_mixed = dot_nt(d_low, mix_ref[...]).astype(BF)
    width = qkv_ref.shape[2] // heads
    pick = rows // 2
    lane = lanes(pick, heads * width)
    allowed = subs(pick, pick) <= lanes(pick, pick)
    dq_parts, dk_parts, dv_parts = [], [], []
    for s in range(2):
        span = slice(s * pick, (s + 1) * pick)
        q, k, v, dm = q_ref[span, :], k_ref[span, :], v_ref[span, :], d_mixed[span]
        dq = jnp.zeros((pick, heads * width), F32)
        dk, dv = dq, dq
        for h in range(heads):
            qh, kh = head_of(q, lane, h, width), head_of(k, lane, h, width)
            dh = head_of(dm, lane, h, width)
            scores = jnp.where(allowed, dot_nt(k, qh), NEGATIVE)
            expos = jnp.exp(scores - jnp.max(scores, axis=0, keepdims=True))
            probs = expos / jnp.sum(expos, axis=0, keepdims=True)
            d_probs = dot_nt(v, dh)
            inner = jnp.sum(probs * d_probs, axis=0, keepdims=True)
            d_scores = (probs * (d_probs - inner)).astype(BF)
            dv = dv + dot(probs.astype(BF), dh)
            dk = dk + dot(d_scores, qh)
            dq = dq + dot_tn(d_scores, kh)
        dq_parts.append(dq * width ** (-0.5))
        dk_parts.append(dk)
        dv_parts.append(dv)
    d_normed = jnp.zeros((rows, d), F32)
    for i, parts in enumerate((dq_parts, dk_parts, dv_parts)):
        whole = jnp.concatenate(parts, 0).astype(BF)
        d_qkv_ref[i] = whole
        d_normed = d_normed + dot_nt(whole, qkv_ref[i])
    unit, _ = unit_rows(picked)
    vec_ref[0:1, :] = jnp.sum(d_normed * unit, axis=0, keepdims=True)
    halves_out(d_normed, low, keep_ref, send_ref)


def routed_back_attn(
    info, own, other, d_sel, picked, attn, both_own, both_other, gains, q, k, v, qkv_w, mix_w, heads
):
    rows, d = picked.shape
    part = shape((2, rows // 4, d), BF)
    return pl.pallas_call(
        functools.partial(routed_back_attn_kernel, heads),
        out_shape=(
            shape((rows, d), F32), shape((rows, d), BF), shape((3,) + q.shape, BF),
            shape((2, d), F32), part, part,
        ),
        in_specs=[SM] + [VM] * 13,
        out_specs=(VM,) * 6,
        compiler_params=params(),
        name="routed_back_attn",
    )(info, own, other, d_sel, picked, attn, both_own, both_other, gains, q, k, v, qkv_w, mix_w)


def finish_kernel(
    info, own_ref, other_ref, d_mid_ref, picked_ref, gains_ref, sel_ref,
    d_rows_ref, far_ref, result_ref, out_ref,
):
    tensor, section, low = info[0], info[1], info[2]
    own = d_rows_ref.shape[0]
    pick = sel_ref.shape[2]

    @pl.when(section == 0)
    def _():
        d_normed = halves_in(own_ref, other_ref, low)
        unit, scale = unit_rows(picked_ref[...].astype(F32))
        d_picked = d_mid_ref[...] + norm_back(unit, scale, gains_ref[0:1, :], d_normed)
        d_picked = d_picked.astype(BF)
        for s in range(2):
            table = (sel_ref[s] == subs(own, pick) + tensor * own).astype(F32).astype(BF)
            base = (d_rows_ref if s == 0 else far_ref)[...].astype(F32)
            out_ref[s] = base + dot(table, d_picked[s * pick : (s + 1) * pick])

    @pl.when(section != 0)
    def _():
        out_ref[0] = far_ref[...].astype(F32)
        out_ref[1] = result_ref[...]


def finish(info, own, other, d_mid, picked, gains, sel_row, d_rows, far, result):
    rows, d = d_rows.shape
    return pl.pallas_call(
        finish_kernel,
        out_shape=shape((2, rows, d), F32),
        in_specs=[SM] + [VM] * 9,
        out_specs=VM,
        compiler_params=params(),
        name="finish",
    )(info, own, other, d_mid, picked, gains, sel_row, d_rows, far, result)


def project_kernel(
    heads, width, info, tok0, tok1, tok2, tok3, upd_own, upd_other, sel_ref, gains_ref, qkv_ref,
    rows_ref, normed_ref, q_ref, k_ref, v_ref, buf,
):
    tensor, low, length = info[0], info[2], info[3]
    r = pl.program_id(0)
    own, d = buf.shape
    for i, tok in enumerate((tok0, tok1, tok2, tok3)):
        @pl.when(r == i)
        def _():
            buf[...] = tok[...]

    place = jnp.bitwise_xor(r, tensor) * own
    pick = sel_ref.shape[1]
    first, second = upd_own[...], upd_other[...]
    update = jnp.concatenate(
        [jnp.where(low == 0, first, second), jnp.where(low == 0, second, first)], 0
    )
    table = (sel_ref[...] == subs(own, pick) + place).astype(F32).astype(BF)
    rows = (buf[...].astype(F32) + dot(table, update)).astype(BF)

    @pl.when(r == 0)
    def _():
        rows_ref[...] = rows

    unit, _ = unit_rows(rows.astype(F32))
    normed = (unit * gains_ref[0:1, :]).astype(BF)
    normed_ref[0] = normed
    lane = lanes(own, PAD)
    cols = heads * width
    one, zero = jnp.float32(1), jnp.float32(0)
    q = dot(normed, qkv_ref[0]).astype(BF).astype(F32) * width ** (-0.5)
    q_ref[0] = jnp.where(lane == cols + 3, one, q).astype(BF)
    key_at = subs(own, PAD) + place
    extra = jnp.where(lane < cols + 3, one, jnp.where(key_at < length, zero, NEGATIVE))
    k = dot(normed, qkv_ref[1])
    k_ref[0] = jnp.where((lane >= cols) & (lane < cols + 4), extra, k).astype(BF)
    v = dot(normed, qkv_ref[2])
    v_ref[0] = jnp.where((lane >= cols) & (lane < cols + 3), one, v).astype(BF)


def project(info, toks, upd_own, upd_other, sel, gains, qkv_w, heads, width):
    own, d = toks[0].shape
    count = len(toks)
    full = lambda dims: pl.BlockSpec(dims, lambda r, info: (0,) * len(dims))
    placed = lambda w: pl.BlockSpec((1, own, w), lambda r, info: (jnp.bitwise_xor(r, info[0]), 0, 0))
    padded = shape((count, own, PAD), BF)
    return pl.pallas_call(
        functools.partial(project_kernel, heads, width),
        out_shape=(shape((own, d), BF), shape((count, own, d), BF), padded, padded, padded),
        grid_spec=pltpu.PrefetchScalarGridSpec(
            num_scalar_prefetch=1,
            grid=(count,),
            in_specs=[full((own, d))] * 4
            + [full(upd_own.shape)] * 2
            + [full(sel.shape), full(gains.shape), full(qkv_w.shape)],
            out_specs=(full((own, d)), placed(d), placed(PAD), placed(PAD), placed(PAD)),
            scratch_shapes=[pltpu.VMEM((own, d), BF)],
        ),
        compiler_params=params(grid=1),
        name="project",
    )(info, *toks, upd_own, upd_other, sel, gains, qkv_w)


def attention_kernel(heads, width, info, q_ref, k_ref, v_ref, mix_ref, part_ref, mixed_ref, lse_ref):
    i = pl.program_id(0)
    block = q_ref.shape[1]
    cols = heads * width
    steps = k_ref.shape[0] // block

    def run(step):
        span = (step + 1) * block
        q = q_ref[0]
        lane = lanes(block, PAD)
        total = jnp.zeros((block, PAD), F32)
        lse = jnp.zeros((block, 128), F32)
        zero = jnp.zeros_like(q)
        for h in range(heads):
            here = (lane >= h * width) & (lane < (h + 1) * width)
            qh = jnp.where(here | (lane == cols + 3), q, zero)
            scores = dot_nt(qh, k_ref[0:span, :])
            causal = lanes(block, block) <= subs(block, block)
            tail = jnp.where(causal, scores[:, span - block :], NEGATIVE)
            high = jnp.max(tail, axis=-1, keepdims=True)
            if step:
                high = jnp.maximum(high, jnp.max(scores[:, : span - block], axis=-1, keepdims=True))
            probs = jnp.exp(tail - high).astype(BF)
            if step:
                probs = jnp.concatenate(
                    [jnp.exp(scores[:, : span - block] - high).astype(BF), probs], 1
                )
            out = dot(probs, v_ref[0:span, :])
            norm = jnp.sum(jnp.where(lane == cols, out, 0.0), axis=-1, keepdims=True)
            total = jnp.where(here, out / norm, total)
            lse = jnp.where(lanes(block, 128) == h, high + jnp.log(norm), lse)
        lse_ref[...] = lse
        mixed = total.astype(BF)
        mixed_ref[...] = mixed
        part_ref[0] = dot(mixed, mix_ref[...]).astype(BF)

    for step in range(steps):
        @pl.when(i == step)
        def _():
            run(step)


def attention(info, q, k, v, mix_w, heads, width, block=256):
    count, own, _ = q.shape
    total = count * own
    d = mix_w.shape[1]
    per = own // block
    k, v = k.reshape(total, PAD), v.reshape(total, PAD)
    full = lambda dims: pl.BlockSpec(dims, lambda i, info: (0,) * len(dims))
    return pl.pallas_call(
        functools.partial(attention_kernel, heads, width),
        out_shape=(shape((count, own, d), BF), shape((total, PAD), BF), shape((total, 128), F32)),
        grid_spec=pltpu.PrefetchScalarGridSpec(
            num_scalar_prefetch=1,
            grid=(total // block,),
            in_specs=[
                pl.BlockSpec((1, block, PAD), lambda i, info: (i // per, i % per, 0)),
                full(k.shape), full(v.shape), full(mix_w.shape),
            ],
            out_specs=(
                pl.BlockSpec(
                    (1, block, d),
                    lambda i, info: (jnp.bitwise_xor(i // per, info[0]), i % per, 0),
                ),
                pl.BlockSpec((block, PAD), lambda i, info: (i, 0)),
                pl.BlockSpec((block, 128), lambda i, info: (i, 0)),
            ),
        ),
        compiler_params=params(grid=1),
        name="attention",
    )(info, q, k, v, mix_w)


def mlp_kernel(
    rows_ref, near_ref, far_ref, cot_ref, gains_ref, up0, up1, up2, up3, dn0, dn1, dn2, dn3,
    result_ref, d_mid_ref, d_mid_low_ref, normed_ref, d_mlp_ref, act_ref, d_pre_ref, vec_ref,
    up_v, down_v, slope_v, sems,
):
    copies = []
    for i, (up, down) in enumerate(((up0, dn0), (up1, dn1), (up2, dn2), (up3, dn3))):
        a = pltpu.make_async_copy(up, up_v.at[i], sems.at[2 * i])
        b = pltpu.make_async_copy(down, down_v.at[i], sems.at[2 * i + 1])
        a.start()
        b.start()
        copies.append((a, b))
    attn = near_ref[...].astype(F32) + far_ref[...].astype(F32)
    middle = rows_ref[...].astype(F32) + attn
    unit2, scale2 = unit_rows(middle)
    normed = (unit2 * gains_ref[1:2, :]).astype(BF)
    normed_ref[...] = normed
    mlp = jnp.zeros_like(middle)
    for i in range(4):
        copies[i][0].wait()
        act, slope = gelu_pair(dot(normed, up_v[i]))
        act = act.astype(BF)
        act_ref[i] = act
        slope_v[i] = slope
        copies[i][1].wait()
        mlp = mlp + dot(act, down_v[i])
    unit3, scale3 = unit_rows(middle + mlp)
    gain3 = gains_ref[2:3, :]
    result_ref[...] = unit3 * gain3
    cot = cot_ref[...].astype(F32)
    vec_ref[1:2, :] = jnp.sum(cot * unit3, axis=0, keepdims=True)
    d_final = norm_back(unit3, scale3, gain3, cot)
    d_mlp = d_final.astype(BF)
    d_mlp_ref[...] = d_mlp
    d_normed = jnp.zeros_like(middle)
    for i in range(4):
        d_pre = (dot_nt(d_mlp, down_v[i]) * slope_v[i]).astype(BF)
        d_pre_ref[i] = d_pre
        d_normed = d_normed + dot_nt(d_pre, up_v[i])
    vec_ref[0:1, :] = jnp.sum(d_normed * unit2, axis=0, keepdims=True)
    d_mid = d_final + norm_back(unit2, scale2, gains_ref[1:2, :], d_normed)
    d_mid_ref[...] = d_mid
    d_mid_low_ref[...] = d_mid.astype(BF)


def mlp_pass(rows, near, far, cot, gains, ups, downs):
    own, d = rows.shape
    hidden = ups[0].shape[1]
    wide, low = shape((own, d), F32), shape((own, d), BF)
    packed = shape((4, own, hidden), BF)
    return pl.pallas_call(
        mlp_kernel,
        out_shape=(wide, wide, low, low, low, packed, packed, shape((2, d), F32)),
        in_specs=[VM] * 5 + [HB] * 8,
        out_specs=(VM,) * 8,
        scratch_shapes=[
            pltpu.VMEM((4, d, hidden), BF),
            pltpu.VMEM((4, hidden, d), BF),
            pltpu.VMEM((4, own, hidden), F32),
            pltpu.SemaphoreType.DMA((8,)),
        ],
        compiler_params=params(60),
        name="dense_mlp",
    )(rows, near, far, cot, gains, *ups, *downs)


def attention_back_kernel(
    heads, width, block, info, g0, g1, g2, g3, q_ref, k_ref, v_ref, mixed_ref, lse_ref, mix_ref,
    qkv_ref, sel_ref, d_qkv_ref, keep_ref, send_ref, qs, ds, dq_acc, dk_acc, dv_acc,
):
    tensor, low = info[0], info[2]
    own = g0.shape[0]
    cols = heads * width
    total = k_ref.shape[0]
    lane = lanes(own, PAD)
    zero = jnp.zeros((own, PAD), BF)
    for r, grad in enumerate((g0, g1, g2, g3)):
        at = pl.multiple_of(jnp.bitwise_xor(tensor, r) * own, own)
        span = pl.ds(at, own)
        d_mixed = dot_nt(grad[...], mix_ref[...]).astype(BF)
        inner = d_mixed.astype(F32) * mixed_ref[span, :].astype(F32)
        q = q_ref[span, :]
        lse = lse_ref[span, :]
        for h in range(heads):
            here = (lane >= h * width) & (lane < (h + 1) * width)
            delta = -jnp.sum(jnp.where(here, inner, 0.0), axis=-1, keepdims=True)
            row_lse = -jnp.sum(jnp.where(lanes(own, 128) == h, lse, 0.0), axis=-1, keepdims=True)
            left = jnp.where(here | (lane == cols + 3), q, zero)
            right = jnp.where(here, d_mixed, zero)
            for p, (a, b) in enumerate(zip(three_pieces(row_lse), three_pieces(delta))):
                left = jnp.where(lane == cols + p, a, left)
                right = jnp.where(lane == cols + p, b, right)
            qs[h, span, :] = left
            ds[h, span, :] = right
    dq_acc[...] = jnp.zeros_like(dq_acc)
    lane_k = lanes(block, PAD)
    allowed = subs(block, block) <= lanes(block, block)
    for j in range(total // block):
        first = j * block
        k, v = k_ref[first : first + block, :], v_ref[first : first + block, :]
        dk_acc[...] = jnp.zeros_like(dk_acc)
        dv_acc[...] = jnp.zeros_like(dv_acc)

        def one_head(h, carry):
            qh, dh = qs[h, first:, :], ds[h, first:, :]
            scores = dot_nt(k, qh)
            d_probs = dot_nt(v, dh)
            head = jnp.where(allowed, scores[:, :block], NEGATIVE)
            probs = jnp.exp(head)
            if first + block < total:
                probs = jnp.concatenate([probs, jnp.exp(scores[:, block:])], 1)
            d_scores = (probs * d_probs).astype(BF)
            dv_acc[...] += dot(probs.astype(BF), dh)
            dk_acc[...] += dot(d_scores, qh)
            kh = jnp.where(
                (lane_k >= h * width) & (lane_k < (h + 1) * width), k, jnp.zeros_like(k)
            )
            dq_acc[first:, :] += dot_tn(d_scores, kh)
            return carry

        lax.fori_loop(0, heads, one_head, 0)
        d_qkv_ref[1, first : first + block, :] = dk_acc[:, :cols].astype(BF)
        d_qkv_ref[2, first : first + block, :] = dv_acc[:, :cols].astype(BF)
    d_qkv_ref[0] = (dq_acc[:, :cols] * width ** (-0.5)).astype(BF)
    pick = sel_ref.shape[0]
    table = (sel_ref[...] == lanes(pick, total)).astype(F32).astype(BF)
    part = jnp.zeros((pick, qkv_ref.shape[1]), F32)
    for i in range(3):
        part = part + dot_nt(dot(table, d_qkv_ref[i]).astype(BF), qkv_ref[i][:, :cols])
    half = pick // 2
    keep_ref[...] = jnp.where(low == 0, part[:half], part[half:]).astype(BF)
    send_ref[...] = jnp.where(low == 0, part[half:], part[:half]).astype(BF)


def attention_back(info, grads, q, k, v, mixed, lse, mix_w, qkv_w, sel_col, heads, width, block=256):
    own, d = grads[0].shape
    total = k.shape[0] * k.shape[1]
    flat = lambda a: a.reshape(total, PAD)
    half = shape((sel_col.shape[0] // 2, d), BF)
    return pl.pallas_call(
        functools.partial(attention_back_kernel, heads, width, block),
        out_shape=(shape((3, total, heads * width), BF), half, half),
        in_specs=[SM] + [VM] * 12,
        out_specs=(VM,) * 3,
        scratch_shapes=[
            pltpu.VMEM((heads, total, PAD), BF),
            pltpu.VMEM((heads, total, PAD), BF),
            pltpu.VMEM((total, PAD), F32),
            pltpu.VMEM((block, PAD), F32),
            pltpu.VMEM((block, PAD), F32),
        ],
        compiler_params=params(60),
        name="attention_back",
    )(info, *grads, flat(q), flat(k), flat(v), mixed, lse, mix_w, qkv_w, sel_col)


def spread_back_kernel(cols, info, d_ref, qkv_ref, out_ref):
    total = dot_nt(d_ref[0, 0], qkv_ref[0][:, :cols])
    for i in (1, 2):
        total = total + dot_nt(d_ref[i, 0], qkv_ref[i][:, :cols])
    out_ref[0] = total.astype(BF)


def spread_back(info, d_qkv, qkv_w, count):
    _, total, cols = d_qkv.shape
    own = total // count
    d = qkv_w.shape[1]
    return pl.pallas_call(
        functools.partial(spread_back_kernel, cols),
        out_shape=shape((count, own, d), BF),
        grid_spec=pltpu.PrefetchScalarGridSpec(
            num_scalar_prefetch=1,
            grid=(count,),
            in_specs=[
                pl.BlockSpec((3, 1, own, cols), lambda a, info: (0, a, 0, 0)),
                pl.BlockSpec(qkv_w.shape, lambda a, info: (0, 0, 0)),
            ],
            out_specs=pl.BlockSpec(
                (1, own, d), lambda a, info: (jnp.bitwise_xor(a, info[0]), 0, 0)
            ),
        ),
        compiler_params=params(grid=1),
        name="spread_back",
    )(info, d_qkv.reshape(3, count, own, cols), qkv_w)


def rows_back_kernel(near_ref, far_ref, rows_ref, d_mid_ref, gains_ref, d_rows_ref, vec_ref):
    d_normed = near_ref[...].astype(F32) + far_ref[...].astype(F32)
    unit, scale = unit_rows(rows_ref[...].astype(F32))
    vec_ref[...] = jnp.sum(d_normed * unit, axis=0, keepdims=True)
    d_rows = d_mid_ref[...] + norm_back(unit, scale, gains_ref[0:1, :], d_normed)
    d_rows_ref[...] = d_rows.astype(BF)


def rows_back(near, far, rows, d_mid, gains):
    own, d = rows.shape
    return pl.pallas_call(
        rows_back_kernel,
        out_shape=(shape((own, d), BF), shape((1, d), F32)),
        in_specs=[VM] * 5,
        out_specs=(VM, VM),
        compiler_params=params(),
        name="rows_back",
    )(near, far, rows, d_mid, gains)


def sel_back_kernel(
    near_ref, far_ref, picked_ref, upd_ref, mid_near, mid_far, gains_ref, out_ref
):
    d_normed = near_ref[...].astype(F32) + far_ref[...].astype(F32)
    rows = (picked_ref[...].astype(F32) + upd_ref[...].astype(F32)).astype(BF).astype(F32)
    unit, scale = unit_rows(rows)
    d_mid = mid_near[...].astype(F32) + mid_far[...].astype(F32)
    out_ref[...] = (d_mid + norm_back(unit, scale, gains_ref[0:1, :], d_normed)).astype(BF)


def sel_back(near, far, picked, upd, mid_near, mid_far, gains):
    return pl.pallas_call(
        sel_back_kernel,
        out_shape=shape(near.shape, BF),
        in_specs=[VM] * 7,
        out_specs=VM,
        compiler_params=params(),
        name="sel_back",
    )(near, far, picked, upd, mid_near, mid_far, gains)


def mid_pick_kernel(info, rows_ref, sel_ref, keep_ref, send_ref):
    tensor, low = info[0], info[2]
    own = rows_ref.shape[0]
    pick = sel_ref.shape[0]
    table = (sel_ref[...] == lanes(pick, own) + tensor * own).astype(F32).astype(BF)
    part = dot(table, rows_ref[...])
    half = pick // 2
    keep_ref[...] = jnp.where(low == 0, part[:half], part[half:]).astype(BF)
    send_ref[...] = jnp.where(low == 0, part[half:], part[:half]).astype(BF)


def mid_pick(info, rows, sel_col):
    out = shape((sel_col.shape[0] // 2, rows.shape[1]), BF)
    return pl.pallas_call(
        mid_pick_kernel,
        out_shape=(out, out),
        in_specs=[SM, VM, VM],
        out_specs=(VM, VM),
        compiler_params=params(),
        name="mid_pick",
    )(info, rows, sel_col)


def add(a, b):
    return (a.astype(F32) + b.astype(F32)).astype(BF)


def core_sum(keep, send):
    return add(keep, swap(send, "tensor", 1))


def whole_sum(keep, send):
    near = core_sum(keep, send)
    return add(near, swap(near, "tensor", 2))


def owner_sum(parts):
    sent = swap(jnp.stack([parts[1], parts[3]]), "tensor", 1)
    far = add(parts[2], sent[1])
    near = add(parts[0], sent[0])
    return near, swap(far, "tensor", 2)


def body(
    tokens, qkv_weight, out_weight, up_weight, down_weight, vectors, lengths, selected, cotangent
):
    section = lax.axis_index("section")
    tensor = lax.axis_index("tensor")
    group = lax.axis_size("dp")
    heads = HEADS // lax.axis_size("tensor")
    low = tensor & 1
    info = jnp.stack([tensor, section, low, lengths[section]]).astype(jnp.int32)
    is_dense = section == 1
    gains = vectors[0]
    qkv_w, mix_w, up_w, down_w = qkv_weight[0], out_weight[0], up_weight[0], down_weight[0]
    cols = qkv_w.shape[2]
    width = cols // heads
    sel_col = selected[:, :, None]
    sel_row = selected[:, None, :]
    my_sel = lax.dynamic_index_in_dim(selected, section, 0, keepdims=False)
    my_col, my_row = my_sel[:, None], my_sel[None, :]

    picked_half = whole_sum(*pick_rows(info, tokens, sel_col))
    picked_other = swap(picked_half, "tensor", 1)

    def dense(own):
        return jnp.where(is_dense, own, hop(own, 1, 0))

    d_gains = dense(gains)
    d_qkv_w = jnp.pad(dense(qkv_w), ((0, 0), (0, 0), (0, PAD - cols)))
    d_mix_w = jnp.pad(dense(mix_w), ((0, PAD - cols), (0, 0)))

    def everywhere(block):
        far = swap(block, "tensor", 2)
        return [block, swap(block, "tensor", 1), far, swap(far, "tensor", 1)]

    my_tokens = lax.dynamic_index_in_dim(tokens, section, 0, keepdims=False)
    toks = everywhere(my_tokens)
    ups = everywhere(dense(up_w))
    downs = everywhere(dense(down_w))

    picked, normed, q, k, v, mixed, keep, send = routed_attn(
        info, picked_half, picked_other, gains, qkv_w, mix_w, heads
    )
    attn_half = whole_sum(keep, send)
    attn_other = swap(attn_half, "tensor", 1)
    attn, normed2, act, slope, keep, send = routed_mlp(
        info, picked, attn_half, attn_other, gains, up_w, down_w
    )
    near = core_sum(keep, send)
    both_half, update_half = make_update(
        picked_half, attn_half, near, swap(near, "tensor", 2), gains
    )
    both_other = swap(both_half, "tensor", 1)
    arrived = hop(update_half[1], 0, 1)
    my_update = jnp.where(is_dense, arrived, update_half[0])
    my_update_other = swap(my_update, "tensor", 1)

    rows, d_normed_rows, dq_in, dk_in, dv_in = project(
        info, toks, my_update, my_update_other, my_row, d_gains, d_qkv_w, heads, width
    )
    parts, d_mixed_rows, lse = attention(info, dq_in, dk_in, dv_in, d_mix_w, heads, width)
    near, far = owner_sum(parts)
    my_cot = lax.dynamic_index_in_dim(cotangent, section, 0, keepdims=False)
    result, d_mid, d_mid_low, m_normed, m_grad, m_act, m_pre, m_vec = mlp_pass(
        rows, near, far, my_cot, d_gains, ups, downs
    )
    grads = everywhere(d_mid_low)
    mid_keep, mid_send = mid_pick(info, d_mid_low, my_col)
    mid_near = core_sum(mid_keep, mid_send)
    mid_far = swap(mid_near, "tensor", 2)
    sent_result = hop(result.astype(BF), 0, 1)

    up_parts = jnp.einsum("rd,frc->fdc", m_normed, m_pre, preferred_element_type=F32).astype(BF)
    down_parts = jnp.einsum("frc,rd->fcd", m_act, m_grad, preferred_element_type=F32).astype(BF)

    d_qkv, keep, send = attention_back(
        info, grads, dq_in, dk_in, dv_in, d_mixed_rows, lse, d_mix_w, d_qkv_w, my_col, heads, width
    )
    near = core_sum(keep, send)
    far = swap(near, "tensor", 2)
    my_picked = lax.dynamic_index_in_dim(picked_half, section, 0, keepdims=False)
    my_d_sel = sel_back(near, far, my_picked, my_update, mid_near, mid_far, d_gains)
    d_sel_half = jnp.stack([my_d_sel, hop(my_d_sel, 1, 0)])
    d_sel_other = swap(d_sel_half, "tensor", 1)

    row_parts = spread_back(info, d_qkv, d_qkv_w, 4)
    near, far = owner_sum(row_parts)
    d_rows, row_vec = rows_back(near, far, rows, d_mid, d_gains)
    flat_normed = d_normed_rows.reshape(-1, d_normed_rows.shape[2])
    qkv_part = jnp.einsum("rd,krc->kdc", flat_normed, d_qkv, preferred_element_type=F32).astype(BF)
    own_count = rows.shape[0]
    mix_part = jnp.zeros((PAD, rows.shape[1]), F32)
    for r in range(4):
        block = lax.dynamic_slice_in_dim(d_mixed_rows, (tensor ^ r) * own_count, own_count, 0)
        mix_part = mix_part + jnp.einsum("rc,rd->cd", block, grads[r], preferred_element_type=F32)
    mix_part = mix_part[:cols].astype(BF)
    near, far = owner_sum(up_parts)
    up_part = add(near, far)
    near, far = owner_sum(down_parts)
    down_part = add(near, far)

    def over_groups(parts):
        qkv_g, mix_g, up_g, down_g = parts
        return (
            lax.psum_scatter(qkv_g, "dp", scatter_dimension=1, tiled=True),
            lax.psum_scatter(mix_g, "dp", scatter_dimension=1, tiled=True),
            lax.psum_scatter(up_g, "dp", scatter_dimension=0, tiled=True),
            lax.psum_scatter(down_g, "dp", scatter_dimension=1, tiled=True),
        )

    dense_sums = over_groups((qkv_part, mix_part, up_part, down_part))
    dense_far = [hop(part, 0, 1) for part in dense_sums]

    d_sel, r_d_mlp, r_d_pre, gain_two, keep, send = routed_back_mlp(
        info, d_sel_half, d_sel_other, picked, attn, gains, slope, up_w, down_w
    )
    half = whole_sum(keep, send)
    other = swap(half, "tensor", 1)
    r_d_mid, r_d_low, r_d_qkv, r_vec, keep, send = routed_back_attn(
        info, half, other, d_sel, picked, attn, both_half, both_other, gains, q, k, v,
        qkv_w, mix_w, heads,
    )
    half = whole_sum(keep, send)
    other = swap(half, "tensor", 1)
    r_up = jnp.einsum("rd,rc->dc", normed2, r_d_pre, preferred_element_type=F32).astype(BF)
    r_down = jnp.einsum("rc,rd->cd", act, r_d_mlp, preferred_element_type=F32).astype(BF)
    r_qkv = jnp.einsum("rd,krc->kdc", normed, r_d_qkv, preferred_element_type=F32).astype(BF)
    r_mix = jnp.einsum("rc,rd->cd", mixed, r_d_low, preferred_element_type=F32).astype(BF)
    routed_sums = over_groups((r_qkv, r_mix, r_up, r_down))

    far_rows = jnp.where(is_dense, sent_result, hop(d_rows, 1, 0))
    combined = finish(
        info, half, other, r_d_mid, picked, gains, sel_row, d_rows, far_rows, result
    )
    final_grads = [
        jnp.where(is_dense, own.astype(F32) + far.astype(F32), routed.astype(F32))
        for own, far, routed in zip(dense_sums, dense_far, routed_sums)
    ]

    vecs = jnp.concatenate([r_vec[0:1], gain_two, r_vec[1:2], row_vec, m_vec], 0)
    for axis in ("tensor", "dp"):
        bit = 1
        while bit < lax.axis_size(axis):
            vecs = vecs + swap(vecs, axis, bit)
            bit *= 2
    dense_vecs = vecs[3:] + hop(vecs[3:], 0, 1)
    vecs = jnp.where(is_dense, dense_vecs, vecs[:3])
    share = vecs.shape[1] // group
    vecs = lax.dynamic_slice_in_dim(vecs, lax.axis_index("dp") * share, share, 1)
    return (
        combined[None],
        final_grads[0][None],
        final_grads[1][None],
        final_grads[2][None],
        final_grads[3][None],
        vecs[None],
    )


def solution(mesh):
    placed = (
        P("dp", "tensor", None),
        P("section", None, None, "tensor"),
        P("section", "tensor", None),
        P("section", None, "tensor"),
        P("section", "tensor", None),
        P("section", None, None),
        P("dp"),
        P("dp", None),
        P("dp", "tensor", None),
    )
    return jax.shard_map(
        body,
        mesh=mesh,
        in_specs=placed,
        out_specs=(
            P("section", "dp", "tensor", None),
            P("section", None, "dp", "tensor"),
            P("section", "tensor", "dp"),
            P("section", "dp", "tensor"),
            P("section", "tensor", "dp"),
            P("section", None, "dp"),
        ),
        check_vma=False,
    )
```

time: 2090 us -> 558 us (0.27)
  matrix products: 778 us -> 23.1 us
  waiting for transfers between devices: 971 us -> 226 us
  Pallas kernels: 0 us -> 139 us
  other arithmetic: 142 us -> 36.8 us
  blocking collectives: 104 us -> 0 us
  starting transfers between devices: 7.51 us -> 54.5 us
    dot_general x128 -> x11, matrix products: 762 us -> 23.1 us  [the longest x1 5.01 us: body(): jnp.einsum('frc,rd->fcd', m_act, m_grad, preferred_element_type=F32)]
    reduce_scatter x28 -> x2, waiting for transfers between devices: 634 us -> 20.9 us  [over_groups(): lax.psum_scatter(up_g, 'dp', scatter_dimension=0, tiled=True)]
    all_gather x8 -> x0, waiting for transfers between devices: 217 us -> none  [the longest x4 111 us: spread_grads(): lax.all_gather(as_sent(values), 'tensor', axis=0, tiled=True)]
    pallas_call x0 -> x15, Pallas kernels: none -> 139 us  [the longest x1 35.7 us: attention_back(): pl.pallas_call(functools.partial(attention_back_kernel, heads, width, blo...]
    ppermute x2 -> x59, waiting for transfers between devices: 71.3 us -> 205 us  [the longest x45 168 us: swap(): return lax.ppermute(block, axis, [(i, i ^ bit) for i in range(count)])]
    all_gather x16 -> x0, blocking collectives: 98.4 us -> none  [the longest x8 49.2 us: spread_rows(): return lax.all_gather(values, 'tensor', axis=0, tiled=True)]
    reduce_sum x30 -> x0, other arithmetic: 62.1 us -> none  [the longest x6 28 us: attention_forward(): totals = jnp.sum(expos, axis=-1, keepdims=True)]
    ppermute x2 -> x59, starting transfers between devices: 4.76 us -> 53.6 us  [the longest x14 30.2 us: hop(): return lax.ppermute(block, 'section', [(source, target)])]
  transfers between devices with their start and end apart: 41 -> 67, of which waited for: 41 -> 30; matrix products, arithmetic and copies ran while one was open for 6% -> 16% of each run, Pallas kernels for 0% -> 19%
where the time goes in v1:
time: 558 us; the launch traced here: 548 us
  waiting for transfers between devices  226 us (41%)
  Pallas kernels  139 us (25%)
  starting transfers between devices  54.5 us (10%)
  local copies, waits for them, and re-layouts  53 us (9%)
  other arithmetic  36.8 us (7%)
  matrix products  23.1 us (4%)
  between operations  15.5 us (3%)
    ppermute x45, waiting for transfers between devices, swap(): return lax.ppermute(block, axis, [(i, i ^ bit) for i in range(count)])  168 us
    ppermute x14, waiting for transfers between devices, hop(): return lax.ppermute(block, 'section', [(source, target)])  36.7 us
    unnamed x169, local copies, waits for them, and re-layouts  36.6 us
    pallas_call x1, Pallas kernels, attention_back(): pl.pallas_call(functools.partial(attention_back_kernel, heads, width, blo...  35.7 us
    ppermute x14, starting transfers between devices, hop(): return lax.ppermute(block, 'section', [(source, target)])  30.2 us
    ppermute x45, starting transfers between devices, swap(): return lax.ppermute(block, axis, [(i, i ^ bit) for i in range(count)])  23.4 us
    pallas_call x1, Pallas kernels, mlp_pass(): pl.pallas_call(mlp_kernel, out_shape=(wide, wide, low, low, low, packed,...  20.9 us
    reduce_scatter x2, waiting for transfers between devices, over_groups(): lax.psum_scatter(up_g, 'dp', scatter_dimension=0, tiled=True)  20.9 us
  transfers between devices with their start and end apart: 67, of which 30 were waited for; matrix products, arithmetic and copies ran while one was open for 16% of the time, Pallas kernels for 19%

profile of v1, /device:TPU:0, one launch (start us, length us, event | category | flops | bytes accessed | tf_op | source)
XLA Modules:
  0.0 548.4 jit_solution(4860374845611720890)
XLA Ops:
  11.4 2.9 pick.1
  17.4 3.0 collective-permute-start.4
  20.4 9.4 %collective-permute-done.4 = bf16[2,128,768]{2,1,0:T(8,128)(2,1)S(1)} collective-permute-done((bf16[2,128,768]{2,1,0:T(8,128)(2,1)S(1)}, bf16[2,128,768]{2,1,0:T(8,128)(2,1)S(1)}, u32[]{:S(2)}, u32[]{:S(2)}) %collective-permute-start.4) | collective-permute-done | bytes 393248 | tf_op jit(solution)/shard_map/ppermute | solution.py:21
  30.6 2.4 copy.37
  33.7 5.2 routed_attn.1
  43.8 9.6 %collective-permute-done.7 = bf16[2,128,768]{2,1,0:T(8,128)(2,1)S(1)} collective-permute-done((bf16[2,128,768]{2,1,0:T(8,128)(2,1)S(1)}, bf16[2,128,768]{2,1,0:T(8,128)(2,1)S(1)}, u32[]{:S(2)}, u32[]{:S(2)}) %collective-permute-start.7) | collective-permute-done | bytes 393248 | tf_op jit(solution)/shard_map/ppermute | solution.py:21
  56.1 5.8 %routed_mlp.1 = (bf16[512,768]{1,0:T(8,128)(2,1)}, bf16[512,768]{1,0:T(8,128)(2,1)}, bf16[512,768]{1,0:T(8,128)(2,1)}, f32[512,768]{1,0:T(8,128)}, bf16[2,128,76...) custom-call(s32[4]{0:T(128)} %pad_add_fusion.info, bf16[512,768]{1,0:T(8,128)(2,1)} %get-tuple-element.63.picked_ref, ...), custom_call_target="tpu_custom_call" | custom-call | tf_op jit(solution)/shard_map/routed_mlp/pallas_call | solution.py:216
  71.5 3.7 collective-permute-done.15
  77.0 9.6 %collective-permute-done.1.tok2 = bf16[512,768]{1,0:T(8,128)(2,1)} collective-permute-done((bf16[512,768]{1,0:T(8,128)(2,1)S(1)}, bf16[512,768]{1,0:T(8,128)(2,1)}, u32[]{:S(2)}, u32[]{:S(2)}) %collective-permute-start.1) | collective-permute-done | bytes 786464 | tf_op jit(solution)/shard_map/ppermute | solution.py:21
  87.9 6.3 %collective-permute-done.14 = bf16[3,768,192]{1,2,0:T(8,128)(2,1)} collective-permute-done((bf16[3,768,192]{1,2,0:T(8,128)(2,1)}, bf16[3,768,192]{1,2,0:T(8,128)(2,1)}, u32[]{:S(2)}, u32[]{:S(2)}) %collective-permute-start.14) | collective-permute-done | bytes 884768 | tf_op jit(solution)/shard_map/ppermute | solution.py:25
  94.2 2.3 copy.39
  96.5 2.6 update.1
  100.1 3.8 collective-permute-start.11
  107.5 11.9 %collective-permute-done.18 = bf16[768,768]{1,0:T(8,128)(2,1)} collective-permute-done((bf16[768,768]{1,0:T(8,128)(2,1)}, bf16[768,768]{1,0:T(8,128)(2,1)}, u32[]{:S(2)}, u32[]{:S(2)}) %collective-permute-start.18) | collective-permute-done | bytes 1179680 | tf_op jit(solution)/shard_map/ppermute | solution.py:25
  123.8 11.1 %project.1 = (bf16[512,768]{1,0:T(8,128)(2,1)}, bf16[4,512,768]{2,1,0:T(8,128)(2,1)}, bf16[4,512,256]{2,1,0:T(8,128)(2,1)}, bf16[4,512,256]{2,1,0:T(8,128)(2,1)}, bf16[4,512,256]{2,1,0:T(8,128)(2,1)}) custom-call(s32[4]{0:T(128)} %pad_add_fusion.info, bf16[512,768]{1,0:T(8,128)(2,1)} %copy-done.19, bf16[512,768]{1,0:T(8,128)(2,1)} %collective-permute-done.tok1, ...), custom_call_target="tpu_custom_call" | custom-call | tf_op jit(solution)/shard_map/project/pallas_call | solution.py:447
  134.9 19.5 %attention.1 = (bf16[4,512,768]{2,1,0:T(8,128)(2,1)}, bf16[2048,256]{1,0:T(8,128)(2,1)}, f32[2048,128]{1,0:T(8,128)}) custom-call(s32[4]{0:T(128)} %pad_add_fusion.info, bf16[4,512,256]{2,1,0:T(8,128)(2,1)} %get-tuple-element.68.q_ref, bf16[2048,256]{1,0:T(8,128)(2,1)} %bitcast.124, bf16[2048,256]{1,0:T(8,128)(2,1)} %bitcast.126, bf16[256,768]{1,0:T(8,128)(2,1)} %pad.9.mix_ref), custom_call_target="tpu_custom_call" | custom-call | tf_op jit(solution)/shard_map/attention/pallas_call | solution.py:513
  159.6 26.4 %collective-permute-done.24.dn2 = bf16[768,768]{1,0:T(8,128)(2,1)S(1)} collective-permute-done((bf16[768,768]{1,0:T(8,128)(2,1)S(1)}, bf16[768,768]{1,0:T(8,128)(2,1)S(1)}, u32[]{:S(2)}, u32[]{:S(2)}) %collective-permute-start.24) | collective-permute-done | bytes 1179680 | tf_op jit(solution)/shard_map/ppermute | solution.py:21
  188.9 18.6 %collective-permute-done.17.far_ref = bf16[512,768]{1,0:T(8,128)(2,1)S(1)} collective-permute-done((bf16[512,768]{1,0:T(8,128)(2,1)S(1)}, bf16[512,768]{1,0:T(8,128)(2,1)S(1)}, u32[]{:S(2)}, u32[]{:S(2)}) %collective-permute-start.17) | collective-permute-done | bytes 786464 | tf_op jit(solution)/shard_map/ppermute | solution.py:21
  208.3 20.9 %dense_mlp.1 = (f32[512,768]{1,0:T(8,128)}, f32[512,768]{1,0:T(8,128)}, bf16[512,768]{1,0:T(8,128)(2,1)}, bf16[512,768]{1,0:T(8,128)(2,1)}, bf16[512,768]{1,0:T(...) custom-call(bf16[512,768]{1,0:T(8,128)(2,1)} %get-tuple-element.67.rows_ref, ...), custom_call_target="tpu_custom_call" | custom-call | tf_op jit(solution)/shard_map/dense_mlp/pallas_call | solution.py:587
  231.1 2.3 mid_pick.1
  234.0 14.7 %collective-permute-done.27.g2 = bf16[512,768]{1,0:T(8,128)(2,1)S(1)} collective-permute-done((bf16[512,768]{1,0:T(8,128)(2,1)}, bf16[512,768]{1,0:T(8,128)(2,1)S(1)}, u32[]{:S(2)}, u32[]{:S(2)}) %collective-permute-start.27) | collective-permute-done | bytes 786464 | tf_op jit(solution)/shard_map/ppermute | solution.py:21
  248.7 5.0 convolution_convert_fusion
  261.2 35.7 %attention_back.1 = (bf16[3,2048,192]{2,1,0:T(8,128)(2,1)}, bf16[128,768]{1,0:T(8,128)(2,1)}, bf16[128,768]{1,0:T(8,128)(2,1)}) custom-call(s32[4]{0:T(128)} %pad_add_fusion.info, bf16[512,768]{1,0:T(8,128)(2,1)} %get-tuple-element.72.g0.rows_ref, bf16[512,768]{1,0:T(8,128)(2,1)} %copy-done.20, bf16[512,768]{1,0:T(8,128)(2,1)} %copy-done.17, ...), custom_call_target="tpu_custom_call" | custom-call | tf_op jit(solution)/shard_map/attention_back/pallas_call | solution.py:676
  300.8 4.2 collective-permute-done.32.mid_far
  305.0 3.5 collective-permute-done.30.far_ref
  309.3 2.3 sel_back.1
  313.4 6.6 %collective-permute-done.33 = bf16[128,768]{1,0:T(8,128)(2,1)S(1)} collective-permute-done((bf16[128,768]{1,0:T(8,128)(2,1)}, bf16[128,768]{1,0:T(8,128)(2,1)S(1)}, u32[]{:S(2)}, u32[]{:S(2)}) %collective-permute-start.33) | collective-permute-done | bytes 196640 | tf_op jit(solution)/shard_map/ppermute | solution.py:25
  323.0 5.6 %routed_back_mlp.1 = (f32[512,768]{1,0:T(8,128)}, bf16[512,768]{1,0:T(8,128)(2,1)}, bf16[512,768]{1,0:T(8,128)(2,1)}, f32[1,768]{1,0:T(1,128)}, bf16[2,128,768]{...) custom-call(s32[4]{0:T(128)} %pad_add_fusion.info, bf16[2,128,768]{2,1,0:T(8,128)(2,1)} %copy-done.30, ...), custom_call_target="tpu_custom_call" | custom-call | tf_op jit(solution)/shard_map/routed_back_mlp/pallas_call | solution.py:275
  329.0 4.0 fusion.3
  334.1 2.3 reshape.77
  340.6 8.0 %collective-permute-done.36 = bf16[2,128,768]{2,1,0:T(8,128)(2,1)S(1)} collective-permute-done((bf16[2,128,768]{2,1,0:T(8,128)(2,1)S(1)}, bf16[2,128,768]{2,1,0:T(8,128)(2,1)S(1)}, u32[]{:S(2)}, u32[]{:S(2)}) %collective-permute-start.36) | collective-permute-done | bytes 393248 | tf_op jit(solution)/shard_map/ppermute | solution.py:21
  351.2 8.2 %routed_back_attn.1 = (f32[512,768]{1,0:T(8,128)}, bf16[512,768]{1,0:T(8,128)(2,1)}, bf16[3,512,192]{2,1,0:T(8,128)(2,1)}, f32[2,768]{1,0:T(2,128)}, bf16[2,128,...) custom-call(s32[4]{0:T(128)} %pad_add_fusion.info, bf16[2,128,768]{2,1,0:T(8,128)(2,1)} %copy-done.31, ...), custom_call_target="tpu_custom_call" | custom-call | tf_op jit(solution)/shard_map/routed_back_attn/pallas_call | solution.py:350
  361.9 11.2 %collective-permute-done.52 = bf16[768,768]{1,0:T(8,128)(2,1)} collective-permute-done((bf16[768,768]{1,0:T(8,128)(2,1)S(1)}, bf16[768,768]{1,0:T(8,128)(2,1)}, u32[]{:S(2)}, u32[]{:S(2)}) %collective-permute-start.52) | collective-permute-done | bytes 1179680 | tf_op jit(solution)/shard_map/ppermute | solution.py:21
  373.1 2.4 fusion
  377.3 4.8 convert_bitcast_fusion
  390.0 2.3 reshape.79
  395.5 7.2 %spread_back.1 = bf16[4,512,768]{2,1,0:T(8,128)(2,1)} custom-call(s32[4]{0:T(128)} %pad_add_fusion.info, bf16[3,4,512,192]{3,2,1,0:T(8,128)(2,1)} %bitcast.128, bf16[3,768,256]{2,1,0:T(8,128)(2,1)} %pad.8.qkv_ref), custom_call_target="tpu_custom_call" | custom-call | tf_op jit(solution)/shard_map/spread_back/pallas_call | solution.py:704
  404.2 19.0 %collective-permute-done.49 = bf16[768,768]{1,0:T(8,128)(2,1)S(1)} collective-permute-done((bf16[768,768]{1,0:T(8,128)(2,1)S(1)}, bf16[768,768]{1,0:T(8,128)(2,1)S(1)}, u32[]{:S(2)}, u32[]{:S(2)}) %collective-permute-start.49) | collective-permute-done | bytes 1179680 | tf_op jit(solution)/shard_map/ppermute | solution.py:21
  423.2 3.1 fusion.1
  426.6 3.4 collective-permute-done.42
  433.6 17.3 %collective-permute-done.43.far_ref = bf16[512,768]{1,0:T(8,128)(2,1)S(1)} collective-permute-done((bf16[512,768]{1,0:T(8,128)(2,1)S(1)}, bf16[512,768]{1,0:T(8,128)(2,1)S(1)}, u32[]{:S(2)}, u32[]{:S(2)}) %collective-permute-start.43) | collective-permute-done | bytes 786464 | tf_op jit(solution)/shard_map/ppermute | solution.py:21
  451.8 4.0 rows_back.1
  463.5 3.5 collective-permute-done.56
  473.0 5.3 collective-permute-start.58
  482.6 5.9 %collective-permute-done.58 = f32[3,768]{1,0:T(4,128)S(1)} collective-permute-done((f32[3,768]{1,0:T(4,128)S(1)}, f32[3,768]{1,0:T(4,128)S(1)}, u32[]{:S(2)}, u32[]{:S(2)}) %collective-permute-start.58) | collective-permute-done | bytes 9248 | tf_op jit(solution)/shard_map/ppermute | solution.py:25
  488.5 5.1 collective-permute-start.46
  504.4 6.1 %finish.1 = f32[2,512,768]{2,1,0:T(8,128)} custom-call(s32[4]{0:T(128)} %pad_add_fusion.info, bf16[2,128,768]{2,1,0:T(8,128)(2,1)} %copy-done.29, bf16[2,128,768]{2,1,0:T(8,128)(2,1)} %copy-done.45, f32[512,768]{1,0:T(8,128)} %get-tuple-element.90.d_mid_ref, bf16[512,768]{1,0:T(8,128)(2,1)} %get-tuple-element.63.picked_ref, f32[3,768]{1,0:T(4,128)} %bitcast.143, ...), custom_call_target="tpu_custom_call" | custom-call | tf_op jit(solution)/shard_map/finish/pallas_call | solution.py:390
  518.5 20.9 %reduce-scatter.23.cloned.1.call-done = bf16[192,768]{1,0:T(8,128)(2,1)} async-done(((bf16[768,768]{1,0:T(8,128)(2,1)}), bf16[192,768]{1,0:T(8,128)(2,1)}) %reduce-scatter.23.cloned.1.call-update) | async-done | bytes 294928 | tf_op jit(solution)/shard_map/reduce_scatter | solution.py:911
  (351 shorter events, 134.0 us)
Async XLA Ops:
  7.2 471.7 %reduce-scatter.29.cloned.1.call-start = ((), (), s32[]{:S(2)}) async-start(), calls=%async_computation.12 | async-start | bytes 491520
  17.4 12.4 %collective-permute-start.4 = (bf16[2,128,768]{2,1,0:T(8,128)(2,1)S(1)}, bf16[2,128,768]{2,1,0:T(8,128)(2,1)S(1)}, u32[]{:S(2)}, u32[]{:S(2)}) collective-permute-start(bf16[2,128,768]{2,1,0:T(8,128)(2,1)S(1)} %add_convert_fusion.16), channel_id=1, source_target_pairs={{0,2},{1,3},{2,0},{3,1},{4,6},{5,7},{6,4},{7,5},{8,10},{9,11},{10,... | collective-permute-start | bytes 1179656 | tf_op jit(solution)/shard_map/ppermute | solution.py:21
  42.0 11.5 %collective-permute-start.7 = (bf16[2,128,768]{2,1,0:T(8,128)(2,1)S(1)}, bf16[2,128,768]{2,1,0:T(8,128)(2,1)S(1)}, u32[]{:S(2)}, u32[]{:S(2)}) collective-permute-start(bf16[2,128,768]{2,1,0:T(8,128)(2,1)S(1)} %add_convert_fusion.14), channel_id=1, source_target_pairs={{0,2},{1,3},{2,0},{3,1},{4,6},{5,7},{6,4},{7,5},{8,10},{9,11},{10,... | collective-permute-start | bytes 1179656 | tf_op jit(solution)/shard_map/ppermute | solution.py:21
  62.1 8.5 %collective-permute-start.13 = (f32[3,768]{1,0:T(4,128)S(1)}, f32[3,768]{1,0:T(4,128)S(1)}, u32[]{:S(2)}, u32[]{:S(2)}) collective-permute-start(f32[3,768]{1,0:T(4,128)S(1)} %bitcast.144), channel_id=1, source_target_pairs={{16,0},{17,1},{18,2},{19,3},{20,4},{21,5},{22,6},{23,7},{24,8},{25... | collective-permute-start | bytes 27656 | tf_op jit(solution)/shard_map/ppermute | solution.py:25
  63.4 11.8 %collective-permute-start.15 = (bf16[192,768]{1,0:T(8,128)(2,1)S(1)}, bf16[192,768]{1,0:T(8,128)(2,1)}, u32[]{:S(2)}, u32[]{:S(2)}) collective-permute-start(bf16[192,768]{1,0:T(8,128)(2,1)S(1)} %bitcast.132), channel_id=1, source_target_pairs={{16,0},{17,1},{18,2},{19,3},{20,4},{21,5},{22,6},{23,7},{24,8},{25... | collective-permute-start | bytes 884744 | tf_op jit(solution)/shard_map/ppermute | solution.py:25
  64.7 29.5 %collective-permute-start.14 = (bf16[3,768,192]{1,2,0:T(8,128)(2,1)}, bf16[3,768,192]{1,2,0:T(8,128)(2,1)}, u32[]{:S(2)}, u32[]{:S(2)}) collective-permute-start(bf16[3,768,192]{1,2,0:T(8,128)(2,1)} %bitcast.11), channel_id=1, source_target_pairs={{16,0},{17,1},{18,2},{19,3},{20,4},{21,5},{22,6},{23,7},{24,8},{25... | collective-permute-start | bytes 2654216 | tf_op jit(solution)/shard_map/ppermute | solution.py:25
  66.1 20.5 %collective-permute-start.1 = (bf16[512,768]{1,0:T(8,128)(2,1)S(1)}, bf16[512,768]{1,0:T(8,128)(2,1)}, u32[]{:S(2)}, u32[]{:S(2)}) collective-permute-start(bf16[512,768]{1,0:T(8,128)(2,1)S(1)} %dynamic-slice_bitcast_fusion.1.tok0), channel_id=1, source_target_pairs={{0,2},{1,3},{2,0},{3,1},{4,6},{5,7},{6,4},{7,5},{8,10},{9,11},{10,... | collective-permute-start | bytes 2359304 | tf_op jit(solution)/shard_map/ppermute | solution.py:21
  68.5 51.0 %collective-permute-start.18 = (bf16[768,768]{1,0:T(8,128)(2,1)}, bf16[768,768]{1,0:T(8,128)(2,1)}, u32[]{:S(2)}, u32[]{:S(2)}) collective-permute-start(bf16[768,768]{1,0:T(8,128)(2,1)} %bitcast.7.up_ref), channel_id=1, source_target_pairs={{16,0},{17,1},{18,2},{19,3},{20,4},{21,5},{22,6},{23,7},{24,8},{25... | collective-permute-start | bytes 3538952 | tf_op jit(solution)/shard_map/ppermute | solution.py:25
  70.6 25.9 %collective-permute-start.10 = (bf16[2,128,768]{2,1,0:T(8,128)(2,1)}, bf16[2,128,768]{2,1,0:T(8,128)(2,1)}, u32[]{:S(2)}, u32[]{:S(2)}) collective-permute-start(bf16[2,128,768]{2,1,0:T(8,128)(2,1)} %add_convert_fusion.12.mlp_ref), channel_id=1, source_target_pairs={{0,2},{1,3},{2,0},{3,1},{4,6},{5,7},{6,4},{7,5},{8,10},{9,11},{10,... | collective-permute-start | bytes 1179656 | tf_op jit(solution)/shard_map/ppermute | solution.py:21
  75.2 47.8 %collective-permute-start = (bf16[512,768]{1,0:T(8,128)(2,1)S(1)}, bf16[512,768]{1,0:T(8,128)(2,1)}, u32[]{:S(2)}, u32[]{:S(2)}) collective-permute-start(bf16[512,768]{1,0:T(8,128)(2,1)S(1)} %dynamic-slice_bitcast_fusion.1.tok0), channel_id=1, source_target_pairs={{0,1},{1,0},{2,3},{3,2},{4,5},{5,4},{6,7},{7,6},{8,9},{9,8},{10,11... | collective-permute-start | bytes 2359304 | tf_op jit(solution)/shard_map/ppermute | solution.py:21
  86.6 69.5 %collective-permute-start.22 = (bf16[768,768]{1,0:T(8,128)(2,1)}, bf16[768,768]{1,0:T(8,128)(2,1)}, u32[]{:S(2)}, u32[]{:S(2)}) collective-permute-start(bf16[768,768]{1,0:T(8,128)(2,1)} %bitcast.118), channel_id=1, source_target_pairs={{16,0},{17,1},{18,2},{19,3},{20,4},{21,5},{22,6},{23,7},{24,8},{25... | collective-permute-start | bytes 3538952 | tf_op jit(solution)/shard_map/ppermute | solution.py:25
  94.2 28.9 %collective-permute-start.2 = (bf16[512,768]{1,0:T(8,128)(2,1)}, bf16[512,768]{1,0:T(8,128)(2,1)}, u32[]{:S(2)}, u32[]{:S(2)}) collective-permute-start(bf16[512,768]{1,0:T(8,128)(2,1)} %collective-permute-done.1.tok2), channel_id=1, source_target_pairs={{0,1},{1,0},{2,3},{3,2},{4,5},{5,4},{6,7},{7,6},{8,9},{9,8},{10,11... | collective-permute-start | bytes 2359304 | tf_op jit(solution)/shard_map/ppermute | solution.py:21
  107.5 15.6 %collective-permute-start.12 = (bf16[128,768]{1,0:T(8,128)(2,1)S(1)}, bf16[128,768]{1,0:T(8,128)(2,1)S(1)}, u32[]{:S(2)}, u32[]{:S(2)}) collective-permute-start(bf16[128,768]{1,0:T(8,128)(2,1)S(1)} %bitcast_select_fusion.upd_own.upd_ref), channel_id=1, source_target_pairs={{0,1},{1,0},{2,3},{3,2},{4,5},{5,4},{6,7},{7,6},{8,9},{9,8},{10,11... | collective-permute-start | bytes 589832 | tf_op jit(solution)/shard_map/ppermute | solution.py:21
  121.2 38.2 %collective-permute-start.20 = (bf16[768,768]{1,0:T(8,128)(2,1)S(1)}, bf16[768,768]{1,0:T(8,128)(2,1)S(1)}, u32[]{:S(2)}, u32[]{:S(2)}) collective-permute-start(bf16[768,768]{1,0:T(8,128)(2,1)S(1)} %broadcast_select_fusion.1.up0), channel_id=1, source_target_pairs={{0,2},{1,3},{2,0},{3,1},{4,6},{5,7},{6,4},{7,5},{8,10},{9,11},{10,... | collective-permute-start | bytes 3538952 | tf_op jit(solution)/shard_map/ppermute | solution.py:21
  156.0 30.0 %collective-permute-start.16 = (bf16[2,512,768]{2,1,0:T(8,128)(2,1)S(1)}, bf16[2,512,768]{2,1,0:T(8,128)(2,1)S(1)}, u32[]{:S(2)}, u32[]{:S(2)}) collective-permute-start(bf16[2,512,768]{2,1,0:T(8,128)(2,1)S(1)} %pad_maximum_fusion.2), channel_id=1, source_target_pairs={{0,1},{1,0},{2,3},{3,2},{4,5},{5,4},{6,7},{7,6},{8,9},{9,8},{10,11... | collective-permute-start | bytes 4718600 | tf_op jit(solution)/shard_map/ppermute | solution.py:21
  158.6 27.4 %collective-permute-start.24 = (bf16[768,768]{1,0:T(8,128)(2,1)S(1)}, bf16[768,768]{1,0:T(8,128)(2,1)S(1)}, u32[]{:S(2)}, u32[]{:S(2)}) collective-permute-start(bf16[768,768]{1,0:T(8,128)(2,1)S(1)} %broadcast_select_fusion.dn0), channel_id=1, source_target_pairs={{0,2},{1,3},{2,0},{3,1},{4,6},{5,7},{6,4},{7,5},{8,10},{9,11},{10,... | collective-permute-start | bytes 3538952 | tf_op jit(solution)/shard_map/ppermute | solution.py:21
  159.0 29.8 %collective-permute-start.19 = (bf16[768,768]{1,0:T(8,128)(2,1)S(1)}, bf16[768,768]{1,0:T(8,128)(2,1)S(1)}, u32[]{:S(2)}, u32[]{:S(2)}) collective-permute-start(bf16[768,768]{1,0:T(8,128)(2,1)S(1)} %broadcast_select_fusion.1.up0), channel_id=1, source_target_pairs={{0,1},{1,0},{2,3},{3,2},{4,5},{5,4},{6,7},{7,6},{8,9},{9,8},{10,11... | collective-permute-start | bytes 3538952 | tf_op jit(solution)/shard_map/ppermute | solution.py:21
  159.0 29.8 %collective-permute-start.23 = (bf16[768,768]{1,0:T(8,128)(2,1)S(1)}, bf16[768,768]{1,0:T(8,128)(2,1)S(1)}, u32[]{:S(2)}, u32[]{:S(2)}) collective-permute-start(bf16[768,768]{1,0:T(8,128)(2,1)S(1)} %broadcast_select_fusion.dn0), channel_id=1, source_target_pairs={{0,1},{1,0},{2,3},{3,2},{4,5},{5,4},{6,7},{7,6},{8,9},{9,8},{10,11... | collective-permute-start | bytes 3538952 | tf_op jit(solution)/shard_map/ppermute | solution.py:21
  159.5 29.3 %collective-permute-start.21 = (bf16[768,768]{1,0:T(8,128)(2,1)S(1)}, bf16[768,768]{1,0:T(8,128)(2,1)S(1)}, u32[]{:S(2)}, u32[]{:S(2)}) collective-permute-start(bf16[768,768]{1,0:T(8,128)(2,1)S(1)} %collective-permute-done.20.up2), channel_id=1, source_target_pairs={{0,1},{1,0},{2,3},{3,2},{4,5},{5,4},{6,7},{7,6},{8,9},{9,8},{10,11... | collective-permute-start | bytes 3538952 | tf_op jit(solution)/shard_map/ppermute | solution.py:21
  187.4 20.0 %collective-permute-start.17 = (bf16[512,768]{1,0:T(8,128)(2,1)S(1)}, bf16[512,768]{1,0:T(8,128)(2,1)S(1)}, u32[]{:S(2)}, u32[]{:S(2)}) collective-permute-start(bf16[512,768]{1,0:T(8,128)(2,1)S(1)} %get-tuple-element.136), channel_id=1, source_target_pairs={{0,2},{1,3},{2,0},{3,1},{4,6},{5,7},{6,4},{7,5},{8,10},{9,11},{10,... | collective-permute-start | bytes 2359304 | tf_op jit(solution)/shard_map/ppermute | solution.py:21
  229.3 19.4 %collective-permute-start.27 = (bf16[512,768]{1,0:T(8,128)(2,1)}, bf16[512,768]{1,0:T(8,128)(2,1)S(1)}, u32[]{:S(2)}, u32[]{:S(2)}) collective-permute-start(bf16[512,768]{1,0:T(8,128)(2,1)} %get-tuple-element.72.g0.rows_ref), channel_id=1, source_target_pairs={{0,2},{1,3},{2,0},{3,1},{4,6},{5,7},{6,4},{7,5},{8,10},{9,11},{10,... | collective-permute-start | bytes 2359304 | tf_op jit(solution)/shard_map/ppermute | solution.py:21
  231.1 29.0 %collective-permute-start.26 = (bf16[512,768]{1,0:T(8,128)(2,1)}, bf16[512,768]{1,0:T(8,128)(2,1)S(1)}, u32[]{:S(2)}, u32[]{:S(2)}) collective-permute-start(bf16[512,768]{1,0:T(8,128)(2,1)} %get-tuple-element.72.g0.rows_ref), channel_id=1, source_target_pairs={{0,1},{1,0},{2,3},{3,2},{4,5},{5,4},{6,7},{7,6},{8,9},{9,8},{10,11... | collective-permute-start | bytes 2359304 | tf_op jit(solution)/shard_map/ppermute | solution.py:21
  233.4 63.7 %collective-permute-start.31 = (bf16[128,768]{1,0:T(8,128)(2,1)}, bf16[128,768]{1,0:T(8,128)(2,1)S(1)}, u32[]{:S(2)}, u32[]{:S(2)}) collective-permute-start(bf16[128,768]{1,0:T(8,128)(2,1)} %get-tuple-element.78), channel_id=1, source_target_pairs={{0,1},{1,0},{2,3},{3,2},{4,5},{5,4},{6,7},{7,6},{8,9},{9,8},{10,11... | collective-permute-start | bytes 589832 | tf_op jit(solution)/shard_map/ppermute | solution.py:21
  248.7 11.4 %collective-permute-start.28 = (bf16[512,768]{1,0:T(8,128)(2,1)S(1)}, bf16[512,768]{1,0:T(8,128)(2,1)S(1)}, u32[]{:S(2)}, u32[]{:S(2)}) collective-permute-start(bf16[512,768]{1,0:T(8,128)(2,1)S(1)} %collective-permute-done.27.g2), channel_id=1, source_target_pairs={{0,1},{1,0},{2,3},{3,2},{4,5},{5,4},{6,7},{7,6},{8,9},{9,8},{10,11... | collective-permute-start | bytes 2359304 | tf_op jit(solution)/shard_map/ppermute | solution.py:21
  257.6 79.3 %collective-permute-start.51 = (bf16[2,768,768]{2,1,0:T(8,128)(2,1)}, bf16[2,768,768]{2,1,0:T(8,128)(2,1)}, u32[]{:S(2)}, u32[]{:S(2)}) collective-permute-start(bf16[2,768,768]{2,1,0:T(8,128)(2,1)} %pad_maximum_fusion.1), channel_id=1, source_target_pairs={{0,1},{1,0},{2,3},{3,2},{4,5},{5,4},{6,7},{7,6},{8,9},{9,8},{10,11... | collective-permute-start | bytes 7077896 | tf_op jit(solution)/shard_map/ppermute | solution.py:21
  299.6 9.0 %collective-permute-start.30 = (bf16[128,768]{1,0:T(8,128)(2,1)S(1)}, bf16[128,768]{1,0:T(8,128)(2,1)S(1)}, u32[]{:S(2)}, u32[]{:S(2)}) collective-permute-start(bf16[128,768]{1,0:T(8,128)(2,1)S(1)} %add_convert_fusion.18.near_ref), channel_id=1, source_target_pairs={{0,2},{1,3},{2,0},{3,1},{4,6},{5,7},{6,4},{7,5},{8,10},{9,11},{10,... | collective-permute-start | bytes 589832 | tf_op jit(solution)/shard_map/ppermute | solution.py:21
  311.6 8.5 %collective-permute-start.33 = (bf16[128,768]{1,0:T(8,128)(2,1)}, bf16[128,768]{1,0:T(8,128)(2,1)S(1)}, u32[]{:S(2)}, u32[]{:S(2)}) collective-permute-start(bf16[128,768]{1,0:T(8,128)(2,1)} %sel_back.1), channel_id=1, source_target_pairs={{16,0},{17,1},{18,2},{19,3},{20,4},{21,5},{22,6},{23,7},{24,8},{25... | collective-permute-start | bytes 589832 | tf_op jit(solution)/shard_map/ppermute | solution.py:25
  321.8 159.4 %reduce-scatter.25.cloned.1.call-start = ((), (), s32[]{:S(2)}) async-start(), calls=%async_computation.10 | async-start | bytes 1228800
  336.4 157.9 %reduce-scatter.31.cloned.1.call-start = ((), (), s32[]{:S(2)}) async-start(), calls=%async_computation.13 | async-start | bytes 491520
  336.5 12.0 %collective-permute-start.36 = (bf16[2,128,768]{2,1,0:T(8,128)(2,1)S(1)}, bf16[2,128,768]{2,1,0:T(8,128)(2,1)S(1)}, u32[]{:S(2)}, u32[]{:S(2)}) collective-permute-start(bf16[2,128,768]{2,1,0:T(8,128)(2,1)S(1)} %add_convert_fusion.11), channel_id=1, source_target_pairs={{0,2},{1,3},{2,0},{3,1},{4,6},{5,7},{6,4},{7,5},{8,10},{9,11},{10,... | collective-permute-start | bytes 1179656 | tf_op jit(solution)/shard_map/ppermute | solution.py:21
  338.8 34.3 %collective-permute-start.52 = (bf16[768,768]{1,0:T(8,128)(2,1)S(1)}, bf16[768,768]{1,0:T(8,128)(2,1)}, u32[]{:S(2)}, u32[]{:S(2)}) collective-permute-start(bf16[768,768]{1,0:T(8,128)(2,1)S(1)} %fusion.8), channel_id=1, source_target_pairs={{0,2},{1,3},{2,0},{3,1},{4,6},{5,7},{6,4},{7,5},{8,10},{9,11},{10,... | collective-permute-start | bytes 3538952 | tf_op jit(solution)/shard_map/ppermute | solution.py:21
  340.6 8.2 %collective-permute-start.38 = (bf16[2,128,768]{2,1,0:T(8,128)(2,1)S(1)}, bf16[2,128,768]{2,1,0:T(8,128)(2,1)S(1)}, u32[]{:S(2)}, u32[]{:S(2)}) collective-permute-start(bf16[2,128,768]{2,1,0:T(8,128)(2,1)S(1)} %copy-done.46), channel_id=1, source_target_pairs={{0,1},{1,0},{2,3},{3,2},{4,5},{5,4},{6,7},{7,6},{8,9},{9,8},{10,11... | collective-permute-start | bytes 1179656 | tf_op jit(solution)/shard_map/ppermute | solution.py:21
  361.8 135.4 %reduce-scatter.33.cloned.1.call-start = ((), (), s32[]{:S(2)}) async-start(), calls=%async_computation.14 | async-start | bytes 1474560
  377.0 125.5 %reduce-scatter.35.cloned.1.call-start = ((), (), s32[]{:S(2)}) async-start(), calls=%async_computation.15 | async-start | bytes 1474560
  388.2 122.3 %reduce-scatter.27.cloned.1.call-start = ((), (), s32[]{:S(2)}) async-start(), calls=%async_computation.11 | async-start | bytes 1228800
  392.3 119.7 %reduce-scatter.21.cloned.1.call-start = ((), (), s32[]{:S(2)}) async-start(), calls=%async_computation.8 | async-start | bytes 1474560 | tf_op jit(solution)/shard_map/reduce_scatter | solution.py:911
  395.1 28.1 %collective-permute-start.49 = (bf16[768,768]{1,0:T(8,128)(2,1)S(1)}, bf16[768,768]{1,0:T(8,128)(2,1)S(1)}, u32[]{:S(2)}, u32[]{:S(2)}) collective-permute-start(bf16[768,768]{1,0:T(8,128)(2,1)S(1)} %fusion.6), channel_id=1, source_target_pairs={{0,2},{1,3},{2,0},{3,1},{4,6},{5,7},{6,4},{7,5},{8,10},{9,11},{10,... | collective-permute-start | bytes 3538952 | tf_op jit(solution)/shard_map/ppermute | solution.py:21
  426.3 113.1 %reduce-scatter.23.cloned.1.call-start = ((), (), s32[]{:S(2)}) async-start(), calls=%async_computation.9 | async-start | bytes 1474560 | tf_op jit(solution)/shard_map/reduce_scatter | solution.py:911
  431.3 19.6 %collective-permute-start.43 = (bf16[512,768]{1,0:T(8,128)(2,1)S(1)}, bf16[512,768]{1,0:T(8,128)(2,1)S(1)}, u32[]{:S(2)}, u32[]{:S(2)}) collective-permute-start(bf16[512,768]{1,0:T(8,128)(2,1)S(1)} %get-tuple-element.134), channel_id=1, source_target_pairs={{0,2},{1,3},{2,0},{3,1},{4,6},{5,7},{6,4},{7,5},{8,10},{9,11},{10,... | collective-permute-start | bytes 2359304 | tf_op jit(solution)/shard_map/ppermute | solution.py:21
  433.5 24.6 %collective-permute-start.39 = (bf16[2,128,768]{2,1,0:T(8,128)(2,1)}, bf16[2,128,768]{2,1,0:T(8,128)(2,1)S(1)}, u32[]{:S(2)}, u32[]{:S(2)}) collective-permute-start(bf16[2,128,768]{2,1,0:T(8,128)(2,1)} %get-tuple-element.89), channel_id=1, source_target_pairs={{0,1},{1,0},{2,3},{3,2},{4,5},{5,4},{6,7},{7,6},{8,9},{9,8},{10,11... | collective-permute-start | bytes 1179656 | tf_op jit(solution)/shard_map/ppermute | solution.py:21
  460.1 35.2 %collective-permute-start.40 = (bf16[2,128,768]{2,1,0:T(8,128)(2,1)S(1)}, bf16[2,128,768]{2,1,0:T(8,128)(2,1)}, u32[]{:S(2)}, u32[]{:S(2)}) collective-permute-start(bf16[2,128,768]{2,1,0:T(8,128)(2,1)S(1)} %add_convert_fusion.9), channel_id=1, source_target_pairs={{0,2},{1,3},{2,0},{3,1},{4,6},{5,7},{6,4},{7,5},{8,10},{9,11},{10,... | collective-permute-start | bytes 1179656 | tf_op jit(solution)/shard_map/ppermute | solution.py:21
  469.9 30.5 %collective-permute-start.44 = (bf16[512,768]{1,0:T(8,128)(2,1)}, bf16[512,768]{1,0:T(8,128)(2,1)S(1)}, u32[]{:S(2)}, u32[]{:S(2)}) collective-permute-start(bf16[512,768]{1,0:T(8,128)(2,1)} %convert_element_type.352), channel_id=1, source_target_pairs={{0,16},{1,17},{2,18},{3,19},{4,20},{5,21},{6,22},{7,23},{8,24},{9,... | collective-permute-start | bytes 2359304 | tf_op jit(solution)/shard_map/ppermute | solution.py:25
  471.5 28.9 %collective-permute-start.45 = (bf16[512,768]{1,0:T(8,128)(2,1)S(1)}, bf16[512,768]{1,0:T(8,128)(2,1)}, u32[]{:S(2)}, u32[]{:S(2)}) collective-permute-start(bf16[512,768]{1,0:T(8,128)(2,1)S(1)} %copy-done.38), channel_id=1, source_target_pairs={{16,0},{17,1},{18,2},{19,3},{20,4},{21,5},{22,6},{23,7},{24,8},{25... | collective-permute-start | bytes 2359304 | tf_op jit(solution)/shard_map/ppermute | solution.py:25
  473.0 15.5 %collective-permute-start.58 = (f32[3,768]{1,0:T(4,128)S(1)}, f32[3,768]{1,0:T(4,128)S(1)}, u32[]{:S(2)}, u32[]{:S(2)}) collective-permute-start(f32[3,768]{1,0:T(4,128)S(1)} %get-tuple-element.142), channel_id=1, source_target_pairs={{0,16},{1,17},{2,18},{3,19},{4,20},{5,21},{6,22},{7,23},{8,24},{9,... | collective-permute-start | bytes 27656 | tf_op jit(solution)/shard_map/ppermute | solution.py:25
  479.8 16.6 %collective-permute-start.47 = (bf16[192,192]{1,0:T(8,128)(2,1)S(1)}, bf16[192,192]{1,0:T(8,128)(2,1)S(1)}, u32[]{:S(2)}, u32[]{:S(2)}) collective-permute-start(bf16[192,192]{1,0:T(8,128)(2,1)S(1)} %copy.61), channel_id=1, source_target_pairs={{0,16},{1,17},{2,18},{3,19},{4,20},{5,21},{6,22},{7,23},{8,24},{9,... | collective-permute-start | bytes 221192 | tf_op jit(solution)/shard_map/ppermute | solution.py:25
  488.5 25.5 %collective-permute-start.46 = (bf16[3,192,192]{1,2,0:T(8,128)(2,1)S(1)}, bf16[3,192,192]{1,2,0:T(8,128)(2,1)}, u32[]{:S(2)}, u32[]{:S(2)}) collective-permute-start(bf16[3,192,192]{1,2,0:T(8,128)(2,1)S(1)} %copy.57), channel_id=1, source_target_pairs={{0,16},{1,17},{2,18},{3,19},{4,20},{5,21},{6,22},{7,23},{8,24},{9,... | collective-permute-start | bytes 663560 | tf_op jit(solution)/shard_map/ppermute | solution.py:25
  498.3 17.8 %collective-permute-start.53 = (bf16[768,192]{1,0:T(8,128)(2,1)S(1)}, bf16[768,192]{1,0:T(8,128)(2,1)}, u32[]{:S(2)}, u32[]{:S(2)}) collective-permute-start(bf16[768,192]{1,0:T(8,128)(2,1)S(1)} %copy.65), channel_id=1, source_target_pairs={{0,16},{1,17},{2,18},{3,19},{4,20},{5,21},{6,22},{7,23},{8,24},{9,... | collective-permute-start | bytes 884744 | tf_op jit(solution)/shard_map/ppermute | solution.py:25
  512.0 27.4 %collective-permute-start.50 = (bf16[192,768]{1,0:T(8,128)(2,1)}, bf16[192,768]{1,0:T(8,128)(2,1)}, u32[]{:S(2)}, u32[]{:S(2)}) collective-permute-start(bf16[192,768]{1,0:T(8,128)(2,1)} %reduce-scatter.21.cloned.1.call-done), channel_id=1, source_target_pairs={{0,16},{1,17},{2,18},{3,19},{4,20},{5,21},{6,22},{7,23},{8,24},{9,... | collective-permute-start | bytes 884744 | tf_op jit(solution)/shard_map/ppermute | solution.py:25
  (94 other events, 933.8 us)
Sparse Core Ops, SparseCore 0:
  321.9 19.9 reduce-scatter.28
  344.4 24.3 reduce-scatter.24
  371.7 19.1 reduce-scatter.30
  393.1 27.4 reduce-scatter.32
  422.9 27.8 reduce-scatter.34
  453.1 25.8 reduce-scatter.26
  481.3 27.7 reduce-scatter.20
  511.5 27.8 reduce-scatter.22
